TPU v7x, 256 devices: a whole 4x4x8 slice. The times are simulated.
256 devices in a mesh: blk: 16 (over x, y_hi, core), help: 16 (over z, y_lo).
Axes of the slice: x: 4, y: 4 (y_hi: 2, y_lo: 2; y = y_hi * 2 + y_lo), z: 8, core: 2. Of those that a mesh axis runs over, the one named last changes fastest.
Arguments:
- queries: bfloat16 [2048, 8192], P('help', 'blk'), may hold values from -200 to 200
- query_key_value: bfloat16 [2048, 2048], P('help'), may hold values from -8 to 8
- cached_key_value: bfloat16 [32768, 2048], P(('blk', 'help')), may hold values from -6 to 6
- selected: int32 [16, 64, 8], P('help'), may hold values from 0 to 31, as said below
Outputs:
- attended: float32 [2048, 8192], P('help', 'blk')
Inputs may be any that keep to these rules, and one draw needn't show every extreme that they name: `selected`: each query block and head selects 8 distinct context blocks, at most one of each run of 2 blocks c * 2 to (c + 1) * 2 - 1.
All inputs are finite; a program needn't handle non-finite values.
Results may differ from a plain program's by a relative error of at most 0.0058.
Values may be sent and summed in bfloat16 or wider, within the bound.
A program may use at most 128 MiB of HBM per device.

v0:
```python
import math

import jax
import jax.numpy as jnp
from jax import lax
from jax.sharding import PartitionSpec as P

HEAD_SIZE = 128
QUERY_HEADS = 64
KEY_VALUE_HEADS = 8
BLOCK_TOKENS = 1024
QUERY_GROUP_ROWS = 128


def from_behind(block, axis, distance):
    devices = range(lax.axis_size(axis))
    route = [((i - distance) % len(devices), i) for i in devices]
    return lax.ppermute(block, axis, route)


def local(queries, query_key_value, cached_key_value, selected):
    rows = queries.shape[0]
    heads_per_unit = queries.shape[1] // HEAD_SIZE
    blocks_per_unit = rows // QUERY_GROUP_ROWS
    head_group = QUERY_HEADS // KEY_VALUE_HEADS
    scale = 1.0 / math.sqrt(HEAD_SIZE)
    nshard = lax.axis_size("blk")
    worker_rank = lax.axis_index("blk")
    quer = queries.reshape(blocks_per_unit, QUERY_GROUP_ROWS, heads_per_unit, HEAD_SIZE)
    fresh_state = query_key_value.reshape(
        blocks_per_unit, QUERY_GROUP_ROWS, 2, KEY_VALUE_HEADS, HEAD_SIZE
    )
    causal = jnp.arange(QUERY_GROUP_ROWS)[:, None] >= jnp.arange(QUERY_GROUP_ROWS)[None, :]

    def attend_block(
        softmax_state, query_portion, leading_head, selection_table, lane_count, shard_piece
    ):
        best_now, total_now, accum_now = softmax_state
        count = query_portion.shape[2]
        key_block = selection_table.shape[0] // lane_count
        picks = lax.dynamic_slice_in_dim(selected, leading_head, count, 1)
        hit = picks // key_block == shard_piece
        local_part = jnp.sum(jnp.where(hit, picks % key_block, 0), axis=2)
        valid = jnp.any(hit, axis=2)
        worker_lanes = (leading_head + jnp.arange(count, dtype=jnp.int32)) // head_group
        block_index = (local_part * lane_count + worker_lanes[None, :]).reshape(-1)
        chosen = jnp.take(selection_table, block_index, axis=0).reshape(
            blocks_per_unit, count, 2, BLOCK_TOKENS, HEAD_SIZE
        )
        scores = (
            jnp.einsum(
                "bqhd,bhsd->bhqs",
                query_portion,
                chosen[:, :, 0],
                preferred_element_type=jnp.float32,
            )
            * scale
        )
        scores = jnp.where(valid[:, :, None, None], scores, -jnp.inf)
        best_new = jnp.maximum(best_now, jnp.max(scores, axis=-1))
        fade = jnp.exp(best_now - best_new)
        weights = jnp.exp(scores - best_new[..., None])
        total_new = total_now * fade + jnp.sum(weights, axis=-1)
        accum_new = accum_now * fade[..., None] + jnp.einsum(
            "bhqs,bhsd->bhqd",
            weights.astype(jnp.bfloat16),
            chosen[:, :, 1],
            preferred_element_type=jnp.float32,
        )
        return (best_new, total_new, accum_new)

    tile_rows = lax.all_gather(cached_key_value, "help", axis=0, tiled=True)
    key_block_list = tile_rows.shape[0] // BLOCK_TOKENS
    arranged_layout = jnp.transpose(
        tile_rows.reshape(key_block_list, BLOCK_TOKENS, 2, KEY_VALUE_HEADS, HEAD_SIZE),
        (0, 3, 2, 1, 4),
    )
    selection_table = arranged_layout.reshape(
        key_block_list * KEY_VALUE_HEADS, 2, BLOCK_TOKENS, HEAD_SIZE
    )
    count = quer.shape[2]
    worker_lanes = (worker_rank * heads_per_unit + jnp.arange(count, dtype=jnp.int32)) // head_group
    own = jnp.take(fresh_state, worker_lanes, axis=3)
    near = (
        jnp.einsum("bqhd,bshd->bhqs", quer, own[:, :, 0], preferred_element_type=jnp.float32)
        * scale
    )
    near = jnp.where(causal[None, None], near, -jnp.inf)
    best = jnp.max(near, axis=-1)
    weight = jnp.exp(near - best[..., None])
    total = jnp.sum(weight, axis=-1)
    accum = jnp.einsum(
        "bhqs,bshd->bhqd",
        weight.astype(jnp.bfloat16),
        own[:, :, 1],
        preferred_element_type=jnp.float32,
    )
    softmax_state = (best, total, accum)

    def forward_step(step, carry):
        inner_loop, moving_part = carry
        owner_rank = (worker_rank - step) % nshard
        inner_loop = attend_block(
            inner_loop,
            moving_part,
            owner_rank * heads_per_unit,
            selection_table,
            KEY_VALUE_HEADS,
            worker_rank,
        )
        moving_part = from_behind(moving_part, "blk", 1)
        inner_loop = from_behind((inner_loop[0], inner_loop[1], inner_loop[2]), "blk", 1)
        return (inner_loop, moving_part)

    softmax_state, moving_part = lax.fori_loop(0, nshard, forward_step, (softmax_state, quer))
    best, total, accum = softmax_state
    result = accum / total[..., None]
    result = jnp.transpose(result, (0, 2, 1, 3)).reshape(rows, heads_per_unit * HEAD_SIZE)
    return result


def solution(mesh):
    in_specs = (P("help", "blk"), P("help", None), P(("blk", "help"), None), P("help", None, None))
    out_specs = P("help", "blk")
    return jax.shard_map(local, mesh=mesh, in_specs=in_specs, out_specs=out_specs, check_vma=False)
```

profile of v0, /device:TPU:1, one launch (start us, length us, event | category | flops | bytes accessed | tf_op | source)
XLA Modules:
  0.0 485.4 jit_solution(13202558709188502187)
XLA Ops:
  11.4 184.1 %all-gather.2.cloned.1.call-done = bf16[2048,2048]{1,0:T(8,128)(2,1)} async-done(((bf16[128,2048]{1,0:T(8,128)(2,1)}), bf16[2048,2048]{1,0:T(8,128)(2,1)}) %all-gather.2.cloned.1.call-update) | async-done | bytes 8388624 | tf_op jit(solution)/shard_map/all_gather | solution.py:72
  195.4 9.7 %copy.33 = bf16[256,8,16,128]{3,2,1,0:T(8,128)(2,1)} copy(bf16[256,8,16,128]{3,1,2,0:T(8,128)(2,1)} %bitcast.118) | data formatting | bytes 16777216
  205.2 8.8 %copy.27 = bf16[2,1024,2,8,128]{4,1,2,3,0:T(8,128)(2,1)} copy(bf16[2,1024,2,8,128]{4,3,2,1,0:T(8,128)(2,1)} %bitcast.117) | data formatting | bytes 16777216 | tf_op jit(solution)/shard_map/reshape | solution.py:75
  214.0 263.5 %while.22 = (s32[]{:T(128)}, f32[1,4,128]{2,1,0:T(4,128)S(1)}, f32[1,4,128]{2,1,0:T(4,128)S(1)}, f32[1,4,128,128]{3,2,1,0:T(8,128)S(1)}, bf16[1,128,4,128]{3,1,2...) while((s32[]{:T(128)}, f32[1,4,128]{2,1,0:T(4,128)S(1)}, ...), condition=%wide.region_7.8_spmd, body=%wide.region_2.0_spmd.sunk | while | flops 275385952 | bytes 19322832 | solution.py:115
  214.0 3.2 collective-permute-start.3
  217.5 4.3 gather_fusion
  225.9 2.7 collective-permute-done.1
  228.6 4.1 collective-permute-start.3
  232.9 4.3 gather_fusion
  239.0 3.9 collective-permute-start.2
  246.2 4.1 collective-permute-start.3
  250.5 4.3 gather_fusion
  261.6 4.1 collective-permute-start.3
  266.0 4.3 gather_fusion
  272.0 3.9 collective-permute-start.2
  279.2 4.1 collective-permute-start.3
  283.5 4.3 gather_fusion
  294.4 4.1 collective-permute-start.3
  298.7 4.3 gather_fusion
  304.7 3.9 collective-permute-start.2
  312.0 4.1 collective-permute-start.3
  316.3 4.3 gather_fusion
  326.7 4.1 collective-permute-start.3
  331.0 4.3 gather_fusion
  337.0 4.9 %collective-permute-start.2 = (f32[1,4,128,128]{3,2,1,0:T(8,128)S(1)}, f32[1,4,128,128]{3,2,1,0:T(8,128)S(1)}, u32[]{:S(2)}, u32[]{:S(2)}) collective-permute-start(f32[1,4,128,128]{3,2,1,0:T(8,128)S(1)} %fusion.47), channel_id=1, source_target_pairs={{240,0},{0,16},{16,32},{32,48},{48,64},{64,80},{80,96},{96,112},{1... | collective-permute-start | bytes 786440 | tf_op jit(solution)/shard_map/while/body/eval_jaxpr/ppermute | solution.py:18
  345.3 4.1 collective-permute-start.3
  349.6 4.3 gather_fusion
  361.2 4.1 collective-permute-start.3
  365.5 4.3 gather_fusion
  371.6 3.4 collective-permute-start.2
  378.4 4.1 collective-permute-start.3
  382.7 4.3 gather_fusion
  394.3 4.1 collective-permute-start.3
  398.6 4.3 gather_fusion
  404.6 3.4 collective-permute-start.2
  408.7 2.7 collective-permute-done.1
  411.4 4.1 collective-permute-start.3
  415.7 4.3 gather_fusion
  427.3 4.1 collective-permute-start.3
  431.6 4.3 gather_fusion
  437.6 3.1 collective-permute-start.2
  444.1 4.1 collective-permute-start.3
  448.5 4.3 gather_fusion
  457.3 2.7 collective-permute-done.1
  460.1 4.1 collective-permute-start.3
  464.4 4.3 gather_fusion
  470.4 3.7 collective-permute-start.2
  474.7 2.7 collective-permute-done.1
  (330 shorter events, 93.8 us)
Async XLA Ops:
  6.5 188.9 %all-gather.2.cloned.1.call-start = ((), (), s32[]{:S(2)}) async-start(), calls=%async_computation | async-start | bytes 8912896 | tf_op jit(solution)/shard_map/all_gather | solution.py:72
  214.0 14.6 %collective-permute-start.3 = (bf16[1,128,4,128]{3,1,2,0:T(8,128)(2,1)S(1)}, bf16[1,128,4,128]{3,1,2,0:T(8,128)(2,1)S(1)}, u32[]{:S(2)}, u32[]{:S(2)}) collective-permute-start(bf16[1,128,4,128]{3,1,2,0:T(8,128)(2,1)S(1)} %copy.56), channel_id=1, source_target_pairs={{240,0},{0,16},{16,32},{32,48},{48,64},{64,80},{80,96},{96,112},{1... | collective-permute-start | bytes 393224 | tf_op jit(solution)/shard_map/while/body/eval_jaxpr/ppermute | solution.py:18
  222.5 3.3 collective-permute-start
  223.5 5.1 %collective-permute-start.2 = (f32[1,4,128,128]{3,2,1,0:T(8,128)S(1)}, f32[1,4,128,128]{3,2,1,0:T(8,128)S(1)}, u32[]{:S(2)}, u32[]{:S(2)}) collective-permute-start(f32[1,4,128,128]{3,2,1,0:T(8,128)S(1)} %fusion.47), channel_id=1, source_target_pairs={{240,0},{0,16},{16,32},{32,48},{48,64},{64,80},{80,96},{96,112},{1... | collective-permute-start | bytes 786440 | tf_op jit(solution)/shard_map/while/body/eval_jaxpr/ppermute | solution.py:18
  228.6 17.6 %collective-permute-start.3 = (bf16[1,128,4,128]{3,1,2,0:T(8,128)(2,1)S(1)}, bf16[1,128,4,128]{3,1,2,0:T(8,128)(2,1)S(1)}, u32[]{:S(2)}, u32[]{:S(2)}) collective-permute-start(bf16[1,128,4,128]{3,1,2,0:T(8,128)(2,1)S(1)} %copy.56), channel_id=1, source_target_pairs={{240,0},{0,16},{16,32},{32,48},{48,64},{64,80},{80,96},{96,112},{1... | collective-permute-start | bytes 393224 | tf_op jit(solution)/shard_map/while/body/eval_jaxpr/ppermute | solution.py:18
  238.0 5.4 %collective-permute-start = (f32[1,4,128]{2,1,0:T(4,128)S(1)}, f32[1,4,128]{2,1,0:T(4,128)S(1)}, u32[]{:S(2)}, u32[]{:S(2)}) collective-permute-start(f32[1,4,128]{2,1,0:T(4,128)S(1)} %get-tuple-element.347), channel_id=1, source_target_pairs={{240,0},{0,16},{16,32},{32,48},{48,64},{64,80},{80,96},{96,112},{1... | collective-permute-start | bytes 6152 | tf_op jit(solution)/shard_map/while/body/eval_jaxpr/ppermute | solution.py:18
  239.0 7.2 %collective-permute-start.2 = (f32[1,4,128,128]{3,2,1,0:T(8,128)S(1)}, f32[1,4,128,128]{3,2,1,0:T(8,128)S(1)}, u32[]{:S(2)}, u32[]{:S(2)}) collective-permute-start(f32[1,4,128,128]{3,2,1,0:T(8,128)S(1)} %fusion.47), channel_id=1, source_target_pairs={{240,0},{0,16},{16,32},{32,48},{48,64},{64,80},{80,96},{96,112},{1... | collective-permute-start | bytes 786440 | tf_op jit(solution)/shard_map/while/body/eval_jaxpr/ppermute | solution.py:18
  246.2 15.4 %collective-permute-start.3 = (bf16[1,128,4,128]{3,1,2,0:T(8,128)(2,1)S(1)}, bf16[1,128,4,128]{3,1,2,0:T(8,128)(2,1)S(1)}, u32[]{:S(2)}, u32[]{:S(2)}) collective-permute-start(bf16[1,128,4,128]{3,1,2,0:T(8,128)(2,1)S(1)} %copy.56), channel_id=1, source_target_pairs={{240,0},{0,16},{16,32},{32,48},{48,64},{64,80},{80,96},{96,112},{1... | collective-permute-start | bytes 393224 | tf_op jit(solution)/shard_map/while/body/eval_jaxpr/ppermute | solution.py:18
  255.6 3.3 collective-permute-start
  256.5 5.1 %collective-permute-start.2 = (f32[1,4,128,128]{3,2,1,0:T(8,128)S(1)}, f32[1,4,128,128]{3,2,1,0:T(8,128)S(1)}, u32[]{:S(2)}, u32[]{:S(2)}) collective-permute-start(f32[1,4,128,128]{3,2,1,0:T(8,128)S(1)} %fusion.47), channel_id=1, source_target_pairs={{240,0},{0,16},{16,32},{32,48},{48,64},{64,80},{80,96},{96,112},{1... | collective-permute-start | bytes 786440 | tf_op jit(solution)/shard_map/while/body/eval_jaxpr/ppermute | solution.py:18
  261.6 17.6 %collective-permute-start.3 = (bf16[1,128,4,128]{3,1,2,0:T(8,128)(2,1)S(1)}, bf16[1,128,4,128]{3,1,2,0:T(8,128)(2,1)S(1)}, u32[]{:S(2)}, u32[]{:S(2)}) collective-permute-start(bf16[1,128,4,128]{3,1,2,0:T(8,128)(2,1)S(1)} %copy.56), channel_id=1, source_target_pairs={{240,0},{0,16},{16,32},{32,48},{48,64},{64,80},{80,96},{96,112},{1... | collective-permute-start | bytes 393224 | tf_op jit(solution)/shard_map/while/body/eval_jaxpr/ppermute | solution.py:18
  271.0 5.5 %collective-permute-start = (f32[1,4,128]{2,1,0:T(4,128)S(1)}, f32[1,4,128]{2,1,0:T(4,128)S(1)}, u32[]{:S(2)}, u32[]{:S(2)}) collective-permute-start(f32[1,4,128]{2,1,0:T(4,128)S(1)} %get-tuple-element.347), channel_id=1, source_target_pairs={{240,0},{0,16},{16,32},{32,48},{48,64},{64,80},{80,96},{96,112},{1... | collective-permute-start | bytes 6152 | tf_op jit(solution)/shard_map/while/body/eval_jaxpr/ppermute | solution.py:18
  272.0 7.2 %collective-permute-start.2 = (f32[1,4,128,128]{3,2,1,0:T(8,128)S(1)}, f32[1,4,128,128]{3,2,1,0:T(8,128)S(1)}, u32[]{:S(2)}, u32[]{:S(2)}) collective-permute-start(f32[1,4,128,128]{3,2,1,0:T(8,128)S(1)} %fusion.47), channel_id=1, source_target_pairs={{240,0},{0,16},{16,32},{32,48},{48,64},{64,80},{80,96},{96,112},{1... | collective-permute-start | bytes 786440 | tf_op jit(solution)/shard_map/while/body/eval_jaxpr/ppermute | solution.py:18
  279.2 15.1 %collective-permute-start.3 = (bf16[1,128,4,128]{3,1,2,0:T(8,128)(2,1)S(1)}, bf16[1,128,4,128]{3,1,2,0:T(8,128)(2,1)S(1)}, u32[]{:S(2)}, u32[]{:S(2)}) collective-permute-start(bf16[1,128,4,128]{3,1,2,0:T(8,128)(2,1)S(1)} %copy.56), channel_id=1, source_target_pairs={{240,0},{0,16},{16,32},{32,48},{48,64},{64,80},{80,96},{96,112},{1... | collective-permute-start | bytes 393224 | tf_op jit(solution)/shard_map/while/body/eval_jaxpr/ppermute | solution.py:18
  288.6 3.0 collective-permute-start
  289.6 4.8 collective-permute-start.2
  294.4 17.6 %collective-permute-start.3 = (bf16[1,128,4,128]{3,1,2,0:T(8,128)(2,1)S(1)}, bf16[1,128,4,128]{3,1,2,0:T(8,128)(2,1)S(1)}, u32[]{:S(2)}, u32[]{:S(2)}) collective-permute-start(bf16[1,128,4,128]{3,1,2,0:T(8,128)(2,1)S(1)} %copy.56), channel_id=1, source_target_pairs={{240,0},{0,16},{16,32},{32,48},{48,64},{64,80},{80,96},{96,112},{1... | collective-permute-start | bytes 393224 | tf_op jit(solution)/shard_map/while/body/eval_jaxpr/ppermute | solution.py:18
  303.8 5.5 %collective-permute-start = (f32[1,4,128]{2,1,0:T(4,128)S(1)}, f32[1,4,128]{2,1,0:T(4,128)S(1)}, u32[]{:S(2)}, u32[]{:S(2)}) collective-permute-start(f32[1,4,128]{2,1,0:T(4,128)S(1)} %get-tuple-element.347), channel_id=1, source_target_pairs={{240,0},{0,16},{16,32},{32,48},{48,64},{64,80},{80,96},{96,112},{1... | collective-permute-start | bytes 6152 | tf_op jit(solution)/shard_map/while/body/eval_jaxpr/ppermute | solution.py:18
  304.7 7.2 %collective-permute-start.2 = (f32[1,4,128,128]{3,2,1,0:T(8,128)S(1)}, f32[1,4,128,128]{3,2,1,0:T(8,128)S(1)}, u32[]{:S(2)}, u32[]{:S(2)}) collective-permute-start(f32[1,4,128,128]{3,2,1,0:T(8,128)S(1)} %fusion.47), channel_id=1, source_target_pairs={{240,0},{0,16},{16,32},{32,48},{48,64},{64,80},{80,96},{96,112},{1... | collective-permute-start | bytes 786440 | tf_op jit(solution)/shard_map/while/body/eval_jaxpr/ppermute | solution.py:18
  312.0 14.7 %collective-permute-start.3 = (bf16[1,128,4,128]{3,1,2,0:T(8,128)(2,1)S(1)}, bf16[1,128,4,128]{3,1,2,0:T(8,128)(2,1)S(1)}, u32[]{:S(2)}, u32[]{:S(2)}) collective-permute-start(bf16[1,128,4,128]{3,1,2,0:T(8,128)(2,1)S(1)} %copy.56), channel_id=1, source_target_pairs={{240,0},{0,16},{16,32},{32,48},{48,64},{64,80},{80,96},{96,112},{1... | collective-permute-start | bytes 393224 | tf_op jit(solution)/shard_map/while/body/eval_jaxpr/ppermute | solution.py:18
  322.3 4.3 collective-permute-start.2
  326.7 18.6 %collective-permute-start.3 = (bf16[1,128,4,128]{3,1,2,0:T(8,128)(2,1)S(1)}, bf16[1,128,4,128]{3,1,2,0:T(8,128)(2,1)S(1)}, u32[]{:S(2)}, u32[]{:S(2)}) collective-permute-start(bf16[1,128,4,128]{3,1,2,0:T(8,128)(2,1)S(1)} %copy.56), channel_id=1, source_target_pairs={{240,0},{0,16},{16,32},{32,48},{48,64},{64,80},{80,96},{96,112},{1... | collective-permute-start | bytes 393224 | tf_op jit(solution)/shard_map/while/body/eval_jaxpr/ppermute | solution.py:18
  336.1 6.5 %collective-permute-start = (f32[1,4,128]{2,1,0:T(4,128)S(1)}, f32[1,4,128]{2,1,0:T(4,128)S(1)}, u32[]{:S(2)}, u32[]{:S(2)}) collective-permute-start(f32[1,4,128]{2,1,0:T(4,128)S(1)} %get-tuple-element.347), channel_id=1, source_target_pairs={{240,0},{0,16},{16,32},{32,48},{48,64},{64,80},{80,96},{96,112},{1... | collective-permute-start | bytes 6152 | tf_op jit(solution)/shard_map/while/body/eval_jaxpr/ppermute | solution.py:18
  337.0 8.3 %collective-permute-start.2 = (f32[1,4,128,128]{3,2,1,0:T(8,128)S(1)}, f32[1,4,128,128]{3,2,1,0:T(8,128)S(1)}, u32[]{:S(2)}, u32[]{:S(2)}) collective-permute-start(f32[1,4,128,128]{3,2,1,0:T(8,128)S(1)} %fusion.47), channel_id=1, source_target_pairs={{240,0},{0,16},{16,32},{32,48},{48,64},{64,80},{80,96},{96,112},{1... | collective-permute-start | bytes 786440 | tf_op jit(solution)/shard_map/while/body/eval_jaxpr/ppermute | solution.py:18
  345.3 15.9 %collective-permute-start.3 = (bf16[1,128,4,128]{3,1,2,0:T(8,128)(2,1)S(1)}, bf16[1,128,4,128]{3,1,2,0:T(8,128)(2,1)S(1)}, u32[]{:S(2)}, u32[]{:S(2)}) collective-permute-start(bf16[1,128,4,128]{3,1,2,0:T(8,128)(2,1)S(1)} %copy.56), channel_id=1, source_target_pairs={{240,0},{0,16},{16,32},{32,48},{48,64},{64,80},{80,96},{96,112},{1... | collective-permute-start | bytes 393224 | tf_op jit(solution)/shard_map/while/body/eval_jaxpr/ppermute | solution.py:18
  354.7 3.8 collective-permute-start
  355.7 5.6 %collective-permute-start.2 = (f32[1,4,128,128]{3,2,1,0:T(8,128)S(1)}, f32[1,4,128,128]{3,2,1,0:T(8,128)S(1)}, u32[]{:S(2)}, u32[]{:S(2)}) collective-permute-start(f32[1,4,128,128]{3,2,1,0:T(8,128)S(1)} %fusion.47), channel_id=1, source_target_pairs={{240,0},{0,16},{16,32},{32,48},{48,64},{64,80},{80,96},{96,112},{1... | collective-permute-start | bytes 786440 | tf_op jit(solution)/shard_map/while/body/eval_jaxpr/ppermute | solution.py:18
  361.2 17.1 %collective-permute-start.3 = (bf16[1,128,4,128]{3,1,2,0:T(8,128)(2,1)S(1)}, bf16[1,128,4,128]{3,1,2,0:T(8,128)(2,1)S(1)}, u32[]{:S(2)}, u32[]{:S(2)}) collective-permute-start(bf16[1,128,4,128]{3,1,2,0:T(8,128)(2,1)S(1)} %copy.56), channel_id=1, source_target_pairs={{240,0},{0,16},{16,32},{32,48},{48,64},{64,80},{80,96},{96,112},{1... | collective-permute-start | bytes 393224 | tf_op jit(solution)/shard_map/while/body/eval_jaxpr/ppermute | solution.py:18
  370.6 5.0 %collective-permute-start = (f32[1,4,128]{2,1,0:T(4,128)S(1)}, f32[1,4,128]{2,1,0:T(4,128)S(1)}, u32[]{:S(2)}, u32[]{:S(2)}) collective-permute-start(f32[1,4,128]{2,1,0:T(4,128)S(1)} %get-tuple-element.347), channel_id=1, source_target_pairs={{240,0},{0,16},{16,32},{32,48},{48,64},{64,80},{80,96},{96,112},{1... | collective-permute-start | bytes 6152 | tf_op jit(solution)/shard_map/while/body/eval_jaxpr/ppermute | solution.py:18
  371.6 6.8 %collective-permute-start.2 = (f32[1,4,128,128]{3,2,1,0:T(8,128)S(1)}, f32[1,4,128,128]{3,2,1,0:T(8,128)S(1)}, u32[]{:S(2)}, u32[]{:S(2)}) collective-permute-start(f32[1,4,128,128]{3,2,1,0:T(8,128)S(1)} %fusion.47), channel_id=1, source_target_pairs={{240,0},{0,16},{16,32},{32,48},{48,64},{64,80},{80,96},{96,112},{1... | collective-permute-start | bytes 786440 | tf_op jit(solution)/shard_map/while/body/eval_jaxpr/ppermute | solution.py:18
  378.4 15.9 %collective-permute-start.3 = (bf16[1,128,4,128]{3,1,2,0:T(8,128)(2,1)S(1)}, bf16[1,128,4,128]{3,1,2,0:T(8,128)(2,1)S(1)}, u32[]{:S(2)}, u32[]{:S(2)}) collective-permute-start(bf16[1,128,4,128]{3,1,2,0:T(8,128)(2,1)S(1)} %copy.56), channel_id=1, source_target_pairs={{240,0},{0,16},{16,32},{32,48},{48,64},{64,80},{80,96},{96,112},{1... | collective-permute-start | bytes 393224 | tf_op jit(solution)/shard_map/while/body/eval_jaxpr/ppermute | solution.py:18
  387.7 3.8 collective-permute-start
  388.7 5.6 %collective-permute-start.2 = (f32[1,4,128,128]{3,2,1,0:T(8,128)S(1)}, f32[1,4,128,128]{3,2,1,0:T(8,128)S(1)}, u32[]{:S(2)}, u32[]{:S(2)}) collective-permute-start(f32[1,4,128,128]{3,2,1,0:T(8,128)S(1)} %fusion.47), channel_id=1, source_target_pairs={{240,0},{0,16},{16,32},{32,48},{48,64},{64,80},{80,96},{96,112},{1... | collective-permute-start | bytes 786440 | tf_op jit(solution)/shard_map/while/body/eval_jaxpr/ppermute | solution.py:18
  394.3 17.1 %collective-permute-start.3 = (bf16[1,128,4,128]{3,1,2,0:T(8,128)(2,1)S(1)}, bf16[1,128,4,128]{3,1,2,0:T(8,128)(2,1)S(1)}, u32[]{:S(2)}, u32[]{:S(2)}) collective-permute-start(bf16[1,128,4,128]{3,1,2,0:T(8,128)(2,1)S(1)} %copy.56), channel_id=1, source_target_pairs={{240,0},{0,16},{16,32},{32,48},{48,64},{64,80},{80,96},{96,112},{1... | collective-permute-start | bytes 393224 | tf_op jit(solution)/shard_map/while/body/eval_jaxpr/ppermute | solution.py:18
  403.7 5.0 %collective-permute-start = (f32[1,4,128]{2,1,0:T(4,128)S(1)}, f32[1,4,128]{2,1,0:T(4,128)S(1)}, u32[]{:S(2)}, u32[]{:S(2)}) collective-permute-start(f32[1,4,128]{2,1,0:T(4,128)S(1)} %get-tuple-element.347), channel_id=1, source_target_pairs={{240,0},{0,16},{16,32},{32,48},{48,64},{64,80},{80,96},{96,112},{1... | collective-permute-start | bytes 6152 | tf_op jit(solution)/shard_map/while/body/eval_jaxpr/ppermute | solution.py:18
  404.6 6.8 %collective-permute-start.2 = (f32[1,4,128,128]{3,2,1,0:T(8,128)S(1)}, f32[1,4,128,128]{3,2,1,0:T(8,128)S(1)}, u32[]{:S(2)}, u32[]{:S(2)}) collective-permute-start(f32[1,4,128,128]{3,2,1,0:T(8,128)S(1)} %fusion.47), channel_id=1, source_target_pairs={{240,0},{0,16},{16,32},{32,48},{48,64},{64,80},{80,96},{96,112},{1... | collective-permute-start | bytes 786440 | tf_op jit(solution)/shard_map/while/body/eval_jaxpr/ppermute | solution.py:18
  411.4 15.9 %collective-permute-start.3 = (bf16[1,128,4,128]{3,1,2,0:T(8,128)(2,1)S(1)}, bf16[1,128,4,128]{3,1,2,0:T(8,128)(2,1)S(1)}, u32[]{:S(2)}, u32[]{:S(2)}) collective-permute-start(bf16[1,128,4,128]{3,1,2,0:T(8,128)(2,1)S(1)} %copy.56), channel_id=1, source_target_pairs={{240,0},{0,16},{16,32},{32,48},{48,64},{64,80},{80,96},{96,112},{1... | collective-permute-start | bytes 393224 | tf_op jit(solution)/shard_map/while/body/eval_jaxpr/ppermute | solution.py:18
  420.8 3.8 collective-permute-start
  421.7 5.6 %collective-permute-start.2 = (f32[1,4,128,128]{3,2,1,0:T(8,128)S(1)}, f32[1,4,128,128]{3,2,1,0:T(8,128)S(1)}, u32[]{:S(2)}, u32[]{:S(2)}) collective-permute-start(f32[1,4,128,128]{3,2,1,0:T(8,128)S(1)} %fusion.47), channel_id=1, source_target_pairs={{240,0},{0,16},{16,32},{32,48},{48,64},{64,80},{80,96},{96,112},{1... | collective-permute-start | bytes 786440 | tf_op jit(solution)/shard_map/while/body/eval_jaxpr/ppermute | solution.py:18
  427.3 16.8 %collective-permute-start.3 = (bf16[1,128,4,128]{3,1,2,0:T(8,128)(2,1)S(1)}, bf16[1,128,4,128]{3,1,2,0:T(8,128)(2,1)S(1)}, u32[]{:S(2)}, u32[]{:S(2)}) collective-permute-start(bf16[1,128,4,128]{3,1,2,0:T(8,128)(2,1)S(1)} %copy.56), channel_id=1, source_target_pairs={{240,0},{0,16},{16,32},{32,48},{48,64},{64,80},{80,96},{96,112},{1... | collective-permute-start | bytes 393224 | tf_op jit(solution)/shard_map/while/body/eval_jaxpr/ppermute | solution.py:18
  436.7 4.7 collective-permute-start
  437.6 6.5 %collective-permute-start.2 = (f32[1,4,128,128]{3,2,1,0:T(8,128)S(1)}, f32[1,4,128,128]{3,2,1,0:T(8,128)S(1)}, u32[]{:S(2)}, u32[]{:S(2)}) collective-permute-start(f32[1,4,128,128]{3,2,1,0:T(8,128)S(1)} %fusion.47), channel_id=1, source_target_pairs={{240,0},{0,16},{16,32},{32,48},{48,64},{64,80},{80,96},{96,112},{1... | collective-permute-start | bytes 786440 | tf_op jit(solution)/shard_map/while/body/eval_jaxpr/ppermute | solution.py:18
  444.1 15.9 %collective-permute-start.3 = (bf16[1,128,4,128]{3,1,2,0:T(8,128)(2,1)S(1)}, bf16[1,128,4,128]{3,1,2,0:T(8,128)(2,1)S(1)}, u32[]{:S(2)}, u32[]{:S(2)}) collective-permute-start(bf16[1,128,4,128]{3,1,2,0:T(8,128)(2,1)S(1)} %copy.56), channel_id=1, source_target_pairs={{240,0},{0,16},{16,32},{32,48},{48,64},{64,80},{80,96},{96,112},{1... | collective-permute-start | bytes 393224 | tf_op jit(solution)/shard_map/while/body/eval_jaxpr/ppermute | solution.py:18
  453.5 3.8 collective-permute-start
  454.5 5.6 %collective-permute-start.2 = (f32[1,4,128,128]{3,2,1,0:T(8,128)S(1)}, f32[1,4,128,128]{3,2,1,0:T(8,128)S(1)}, u32[]{:S(2)}, u32[]{:S(2)}) collective-permute-start(f32[1,4,128,128]{3,2,1,0:T(8,128)S(1)} %fusion.47), channel_id=1, source_target_pairs={{240,0},{0,16},{16,32},{32,48},{48,64},{64,80},{80,96},{96,112},{1... | collective-permute-start | bytes 786440 | tf_op jit(solution)/shard_map/while/body/eval_jaxpr/ppermute | solution.py:18
  460.1 17.4 %collective-permute-start.3 = (bf16[1,128,4,128]{3,1,2,0:T(8,128)(2,1)S(1)}, bf16[1,128,4,128]{3,1,2,0:T(8,128)(2,1)S(1)}, u32[]{:S(2)}, u32[]{:S(2)}) collective-permute-start(bf16[1,128,4,128]{3,1,2,0:T(8,128)(2,1)S(1)} %copy.56), channel_id=1, source_target_pairs={{240,0},{0,16},{16,32},{32,48},{48,64},{64,80},{80,96},{96,112},{1... | collective-permute-start | bytes 393224 | tf_op jit(solution)/shard_map/while/body/eval_jaxpr/ppermute | solution.py:18
  469.4 5.3 %collective-permute-start = (f32[1,4,128]{2,1,0:T(4,128)S(1)}, f32[1,4,128]{2,1,0:T(4,128)S(1)}, u32[]{:S(2)}, u32[]{:S(2)}) collective-permute-start(f32[1,4,128]{2,1,0:T(4,128)S(1)} %get-tuple-element.347), channel_id=1, source_target_pairs={{240,0},{0,16},{16,32},{32,48},{48,64},{64,80},{80,96},{96,112},{1... | collective-permute-start | bytes 6152 | tf_op jit(solution)/shard_map/while/body/eval_jaxpr/ppermute | solution.py:18
  470.4 7.1 %collective-permute-start.2 = (f32[1,4,128,128]{3,2,1,0:T(8,128)S(1)}, f32[1,4,128,128]{3,2,1,0:T(8,128)S(1)}, u32[]{:S(2)}, u32[]{:S(2)}) collective-permute-start(f32[1,4,128,128]{3,2,1,0:T(8,128)S(1)} %fusion.47), channel_id=1, source_target_pairs={{240,0},{0,16},{16,32},{32,48},{48,64},{64,80},{80,96},{96,112},{1... | collective-permute-start | bytes 786440 | tf_op jit(solution)/shard_map/while/body/eval_jaxpr/ppermute | solution.py:18
  (19 other events, 61.0 us)
Sparse Core Ops, SparseCore 0:
  9.1 186.2 all-gather.1
where the time goes:
time: 488 us; the launch traced here: 485 us
  waiting for transfers between devices  228 us (47%)
  starting transfers between devices  113 us (23%)
  local copies, waits for them, and re-layouts  92.3 us (19%)
  matrix products  20.9 us (4%)
  other arithmetic  16.5 us (3%)
  between operations  13.5 us (3%)
    all_gather x1, waiting for transfers between devices, local(): tile_rows = lax.all_gather(cached_key_value, 'help', axis=0, tiled=True)  184 us
    ppermute x64, starting transfers between devices, from_behind(): return lax.ppermute(block, axis, route)  113 us
    gather x16, local copies, waits for them, and re-layouts, attend_block(): jnp.take(selection_table, block_index, axis=0)  69.3 us
    ppermute x64, waiting for transfers between devices, from_behind(): return lax.ppermute(block, axis, route)  43.5 us
    dot_general x16, matrix products, attend_block(): jnp.einsum('bhqs,bhsd->bhqd', weights.astype(jnp.bfloat16), chosen[:, :,...  13.2 us
    unnamed x8, local copies, waits for them, and re-layouts  12.8 us
  transfers between devices with their start and end apart: 65, of which 17 were waited for; matrix products, arithmetic and copies ran while one was open for 23% of the time, Pallas kernels for 0%

commit v1 on v0

v1 whole, which is shorter than its diff:
```python
import math

import jax
import jax.numpy as jnp
from jax import lax
from jax.experimental import pallas as pl
from jax.experimental.pallas import tpu as pltpu
from jax.sharding import PartitionSpec as P

D = 128
R = 128
G = 8
NZ = 8
TOPK = 8
HEADS = 4
PAIRS = 16
PLANE = 16
FAR = -1e9
SCALE = math.log2(math.e) / math.sqrt(D)
MESH = pl.DeviceIdType.MESH
NT = (((1,), (1,)), ((), ()))


def remote(src, dst, send, recv, blk, hlp):
    return pltpu.make_async_remote_copy(
        src_ref=src, dst_ref=dst, send_sem=send, recv_sem=recv,
        device_id={"blk": blk, "help": hlp}, device_id_type=MESH,
    )


def kernel(
    q_ref, kv_ref, sel_ref, own_ref, out_ref,
    vts, kbuf, vbuf, qbuf, selv, sels, ownk, ownv, scores, part, stats, near, nstat,
    out_o, in_o, out_s, in_s,
    loc_sem, k_send, k_recv, v_send, v_recv, f_send, fk_recv, fv_recv,
    q_send, q_recv, s_send, s_recv, o_send, o_recv, t_send, t_recv,
):
    i = lax.axis_index("blk")
    j = lax.axis_index("help")
    g, u = i // 2, i % 2
    z, ylo = j // 2, j % 2
    me = 2 * g + ylo
    right = 2 * ((z + 1) % NZ) + ylo
    left = 2 * ((z + NZ - 1) % NZ) + ylo
    sib = 2 * g + (1 - u)

    def plane_of(t):
        return 2 * (t // 2) + u, 2 * z + t % 2

    gcol = pl.multiple_of(g * D, D)
    own_k_copy = pltpu.make_async_copy(own_ref.at[:, pl.ds(gcol, D)], ownk, loc_sem.at[0])
    own_v_copy = pltpu.make_async_copy(
        own_ref.at[:, pl.ds(pl.multiple_of(G * D + g * D, D), D)], ownv, loc_sem.at[1]
    )
    own_k_copy.start()
    own_v_copy.start()

    barrier = pltpu.get_barrier_semaphore()

    def greet_plane(k, c):
        b, h = plane_of((me + k) % PLANE)
        pl.semaphore_signal(barrier, inc=1, device_id={"blk": b, "help": h}, device_id_type=MESH)
        return c

    def greet_ring(k, c):
        h = 2 * ((z + k) % NZ) + ylo
        pl.semaphore_signal(barrier, inc=1, device_id={"blk": i, "help": h}, device_id_type=MESH)
        return c

    lax.fori_loop(1, PLANE, greet_plane, 0)
    lax.fori_loop(1, NZ, greet_ring, 0)
    pl.semaphore_signal(barrier, inc=1, device_id={"blk": sib, "help": j}, device_id_type=MESH)
    pl.semaphore_wait(barrier, PLANE - 1 + NZ - 1 + 1)

    def q_copy(way, s, half):
        block = (z - (s - 1)) % NZ if way == 0 else (z + (s - 1)) % NZ
        rows = pl.ds(half * (R // 2), R // 2)
        src = q_ref.at[rows, :] if s == 1 else qbuf.at[block, rows, :]
        return remote(
            src, qbuf.at[block, rows, :], q_send.at[way, s - 1, half], q_recv.at[way, s - 1, half],
            i, right if way == 0 else left,
        )

    def q_halves(s):
        return [(w, h) for h in (0, 1) for w in (0, 1) if s < 4 or w == h]

    for w, h in q_halves(1):
        q_copy(w, 1, h).start()

    def k_copy(k):
        t = (me + k) % PLANE
        b, h = plane_of(t)
        col = pl.multiple_of((t // 2) * D, D)
        return remote(
            kv_ref.at[:, pl.ds(col, D)], kbuf.at[i, ylo], k_send.at[k], k_recv.at[me], b, h
        )

    def v_copy(k):
        t = (me + k) % PLANE
        b, h = plane_of(t)
        return remote(vts.at[t // 2], vbuf.at[i, ylo], v_send.at[k], v_recv.at[me], b, h)

    lax.fori_loop(1, PLANE, lambda k, c: (k_copy(k).start(), c)[1], 0)
    for head in range(G):
        vts[head] = jnp.transpose(kv_ref[:, (G + head) * D : (G + head + 1) * D])
    lax.fori_loop(1, PLANE, lambda k, c: (v_copy(k).start(), c)[1], 0)

    def s_copy(k):
        h = 2 * ((z + k) % NZ) + ylo
        rows = pl.ds(pl.multiple_of(g * 8, 8), 8)
        return remote(sel_ref.at[0, rows, :], selv.at[z], s_send.at[k], s_recv.at[z], i, h)

    lax.fori_loop(1, NZ, lambda k, c: (s_copy(k).start(), c)[1], 0)
    selv[z] = sel_ref[0, pl.ds(pl.multiple_of(g * 8, 8), 8), :]
    qbuf[z] = q_ref[...]
    kbuf[i, ylo] = kv_ref[:, pl.ds(gcol, D)]
    vbuf[i, ylo] = vts[g]

    def forward(s):
        pair = 2 * (s // 2) + u
        slot = s % 2
        return (
            remote(kbuf.at[pair, slot], kbuf.at[pair, slot], f_send.at[0, s], fk_recv.at[s], sib, j),
            remote(vbuf.at[pair, slot], vbuf.at[pair, slot], f_send.at[1, s], fv_recv.at[s], sib, j),
        )

    for copy in forward(me):
        copy.start()

    own_k_copy.wait()
    own_v_copy.wait()
    causal = lax.broadcasted_iota(jnp.int32, (R, R), 0) <= lax.broadcasted_iota(jnp.int32, (R, R), 1)
    own_vt = jnp.transpose(ownv[...])
    for h in range(HEADS):
        s = lax.dot_general(ownk[...], q_ref[:, h * D : (h + 1) * D], NT, preferred_element_type=jnp.float32)
        s = jnp.where(causal, s, FAR)
        top = jnp.max(s, axis=0, keepdims=True)
        w = jnp.exp2((s - top) * SCALE)
        nstat[h : h + 1] = top
        nstat[HEADS + h : HEADS + h + 1] = jnp.sum(w, axis=0, keepdims=True)
        near[h] = jnp.dot(own_vt, w.astype(jnp.bfloat16), preferred_element_type=jnp.float32)

    def arrive(k, c):
        s = (me + PLANE - k) % PLANE
        pair = 2 * (s // 2) + u
        slot = s % 2
        to_k, to_v = forward(s)
        remote(kbuf.at[pair, slot], kbuf.at[pair, slot], k_send.at[k], k_recv.at[s], i, j).wait_recv()
        to_k.start()
        remote(vbuf.at[pair, slot], vbuf.at[pair, slot], v_send.at[k], v_recv.at[s], i, j).wait_recv()
        to_v.start()
        return c

    def q_arrived(way, s, half):
        block = (z - s) % NZ if way == 0 else (z + s) % NZ
        rows = pl.ds(half * (R // 2), R // 2)
        remote(
            qbuf.at[block, rows, :], qbuf.at[block, rows, :], q_send.at[way, s - 1, half],
            q_recv.at[way, s - 1, half], i, right,
        ).wait_recv()

    for s, (lo, hi) in zip((1, 2, 3), ((1, 5), (5, 9), (9, 13))):
        lax.fori_loop(lo, hi, arrive, 0)
        ahead = q_halves(s + 1)
        for w, h in q_halves(s):
            q_arrived(w, s, h)
            if (w, h) in ahead:
                q_copy(w, s + 1, h).start()
    lax.fori_loop(13, PLANE, arrive, 0)
    for w, h in q_halves(4):
        q_arrived(w, 4, h)

    def from_sibling(s, c):
        pair = 2 * (s // 2) + (1 - u)
        slot = s % 2
        remote(kbuf.at[pair, slot], kbuf.at[pair, slot], f_send.at[0, s], fk_recv.at[s], sib, j).wait_recv()
        remote(vbuf.at[pair, slot], vbuf.at[pair, slot], f_send.at[1, s], fv_recv.at[s], sib, j).wait_recv()
        return c

    lax.fori_loop(0, PLANE, from_sibling, 0)

    def picks_arrived(k, c):
        zs = (z + NZ - k) % NZ
        remote(selv.at[zs], selv.at[zs], s_send.at[k], s_recv.at[zs], i, j).wait_recv()
        return c

    lax.fori_loop(1, NZ, picks_arrived, 0)
    to_smem = pltpu.make_async_copy(selv, sels, loc_sem.at[2])
    to_smem.start()
    to_smem.wait()

    parity = z // (NZ // 2)

    def attend(b):
        def first(h):
            q = qbuf[b, :, h * D : (h + 1) * D]
            top = jnp.full((1, R), 4 * FAR, jnp.float32)
            for t in range(TOPK):
                c = sels[b, HEADS * u + h, t]
                k = kbuf[c // 2].reshape(2 * R, D)
                s = lax.dot_general(k, q, NT, preferred_element_type=jnp.float32)
                s = s + jnp.where(c % 2 == parity, 0.0, FAR)
                scores[h % 2, t] = s
                top = jnp.maximum(top, jnp.max(s, axis=0, keepdims=True))
            return top

        def second(h, top):
            total = jnp.zeros((1, R), jnp.float32)
            acc = jnp.zeros((D, R), jnp.float32)
            for t in range(TOPK):
                c = sels[b, HEADS * u + h, t]
                w = jnp.exp2((scores[h % 2, t] - top) * SCALE)
                total = total + jnp.sum(w, axis=0, keepdims=True)
                v = jnp.concatenate([vbuf[c // 2, 0], vbuf[c // 2, 1]], axis=1)
                acc = acc + jnp.dot(v, w.astype(jnp.bfloat16), preferred_element_type=jnp.float32)
            part[b, h] = acc
            stats[b, h : h + 1] = top
            stats[b, HEADS + h : HEADS + h + 1] = total

        top = first(0)
        for h in range(HEADS):
            after = first(h + 1) if h + 1 < HEADS else None
            second(h, top)
            top = after

    def merge(a, b):
        (ma, la, oa), (mb, lb, ob) = a, b
        m = jnp.maximum(ma, mb)
        fa, fb = jnp.exp2((ma - m) * SCALE), jnp.exp2((mb - m) * SCALE)
        return m, la * fa + lb * fb, oa * fa + ob * fb

    def mine(b, h):
        return stats[b, h : h + 1], stats[b, HEADS + h : HEADS + h + 1], part[b, h]

    def came(way, s, h):
        c, r = h // 2, h % 2
        return (
            in_s[way, s, c, r : r + 1], in_s[way, s, c, 2 + r : 3 + r],
            in_o[way, s, h].astype(jnp.float32),
        )

    def back(way, s, c):
        heads = pl.ds(2 * c, 2)
        hlp = right if way == 0 else left
        return (
            remote(out_o.at[way, s, heads], in_o.at[way, s, heads], o_send.at[way, s, c], o_recv.at[way, s, c], i, hlp),
            remote(out_s.at[way, s, c], in_s.at[way, s, c], t_send.at[way, s, c], t_recv.at[way, s, c], i, hlp),
        )

    def sends(way, s, c):
        return s >= 1 or c == way

    for s in range(4):
        ahead = (z + 4 - s) % NZ
        behind = z if s == 0 else (z + 4 + s) % NZ
        lax.fori_loop(0, 2, lambda n, c: (attend(jnp.where(n == 0, ahead, behind)), c)[1], 0)
        for c in (0, 1):
            for way in (0, 1):
                if not sends(way, s, c):
                    continue
                if s >= 1 and sends(way, s - 1, c):
                    for copy in back(way, s - 1, c):
                        copy.wait_recv()
                b = ahead if way == 0 or s == 0 else behind
                for h in (2 * c, 2 * c + 1):
                    state = mine(b, h)
                    if s >= 1 and sends(way, s - 1, c):
                        state = merge(state, came(way, s - 1, h))
                    r = h % 2
                    out_s[way, s, c, r : r + 1] = state[0]
                    out_s[way, s, c, 2 + r : 3 + r] = state[1]
                    out_o[way, s, h] = state[2].astype(jnp.bfloat16)
                for copy in back(way, s, c):
                    copy.start()

    for h in range(HEADS):
        part[z, h], stats[z, h : h + 1], stats[z, HEADS + h : HEADS + h + 1] = (
            lambda m: (m[2], m[0], m[1])
        )(merge(mine(z, h), (nstat[h : h + 1], nstat[HEADS + h : HEADS + h + 1], near[h])))
    for c in (0, 1):
        for way in (0, 1):
            for copy in back(way, 3, c):
                copy.wait_recv()
        for h in (2 * c, 2 * c + 1):
            state = merge(merge(mine(z, h), came(0, 3, h)), came(1, 3, h))
            out_ref[:, h * D : (h + 1) * D] = jnp.transpose(state[2] / state[1])

    for s in range(1, 5):
        for w, h in q_halves(s):
            q_copy(w, s, h).wait_send()
    lax.fori_loop(1, PLANE, lambda k, c: (k_copy(k).wait_send(), v_copy(k).wait_send(), c)[2], 0)
    lax.fori_loop(1, NZ, lambda k, c: (s_copy(k).wait_send(), c)[1], 0)
    lax.fori_loop(0, PLANE, lambda k, c: ([x.wait_send() for x in forward(k)], c)[1], 0)
    for s in range(4):
        for c in (0, 1):
            for way in (0, 1):
                if sends(way, s, c):
                    for copy in back(way, s, c):
                        copy.wait_send()


def local(queries, query_key_value, cached_key_value, selected):
    bf16, f32 = jnp.bfloat16, jnp.float32
    dma = pltpu.SemaphoreType.DMA
    vmem = pl.BlockSpec(memory_space=pltpu.VMEM)
    return pl.pallas_call(
        kernel,
        out_shape=jax.ShapeDtypeStruct((R, HEADS * D), f32),
        in_specs=[vmem, vmem, vmem, pl.BlockSpec(memory_space=pl.ANY)],
        out_specs=vmem,
        scratch_shapes=[
            pltpu.VMEM((G, D, R), bf16),
            pltpu.VMEM((PAIRS, 2, R, D), bf16),
            pltpu.VMEM((PAIRS, 2, D, R), bf16),
            pltpu.VMEM((NZ, R, HEADS * D), bf16),
            pltpu.VMEM((NZ, 8, TOPK), jnp.int32),
            pltpu.SMEM((NZ, 8, TOPK), jnp.int32),
            pltpu.VMEM((R, D), bf16),
            pltpu.VMEM((R, D), bf16),
            pltpu.VMEM((2, TOPK, 2 * R, R), f32),
            pltpu.VMEM((NZ, HEADS, D, R), f32),
            pltpu.VMEM((NZ, 2 * HEADS, R), f32),
            pltpu.VMEM((HEADS, D, R), f32),
            pltpu.VMEM((2 * HEADS, R), f32),
            pltpu.VMEM((2, 4, HEADS, D, R), bf16),
            pltpu.VMEM((2, 4, HEADS, D, R), bf16),
            pltpu.VMEM((2, 4, 2, 8, R), f32),
            pltpu.VMEM((2, 4, 2, 8, R), f32),
            dma((3,)),
            dma((PLANE,)), dma((PLANE,)), dma((PLANE,)), dma((PLANE,)),
            dma((2, PLANE)), dma((PLANE,)), dma((PLANE,)),
            dma((2, 4, 2)), dma((2, 4, 2)),
            dma((NZ,)), dma((NZ,)),
            dma((2, 4, 2)), dma((2, 4, 2)), dma((2, 4, 2)), dma((2, 4, 2)),
        ],
        compiler_params=pltpu.CompilerParams(
            collective_id=0, has_side_effects=True, vmem_limit_bytes=40 * 2**20
        ),
    )(queries, cached_key_value, selected, query_key_value)


def solution(mesh):
    in_specs = (P("help", "blk"), P("help", None), P(("blk", "help"), None), P("help", None, None))
    return jax.shard_map(
        local, mesh=mesh, in_specs=in_specs, out_specs=P("help", "blk"), check_vma=False
    )
```

time: 488 us -> 64 us (0.13)
  the two profiles are of different devices: /device:TPU:1 before, /device:TPU:18 now
where the time goes in v1:
time: 64 us; the launch traced here: 63.8 us
  Pallas kernels  59.3 us (93%)
  local copies, waits for them, and re-layouts  4.46 us (7%)
    pallas_call x1, Pallas kernels, local(): pl.pallas_call(kernel, out_shape=jax.ShapeDtypeStruct((R, HEADS * D), f32...  59.3 us
    unnamed x8, local copies, waits for them, and re-layouts  4.46 us

profile of v1, /device:TPU:18, one launch (start us, length us, event | category | flops | bytes accessed | tf_op | source)
XLA Modules:
  0.0 63.8 jit_solution(17580055858488786437)
XLA Ops:
  0.0 0.8 %copy.5.sel_ref = s32[1,64,8]{2,1,0:T(8,128)S(1)} copy(s32[1,64,8]{1,2,0:T(8,128)} %param.7) | data formatting | bytes 4096 | tf_op args[3]
  0.8 0.0 copy-start
  0.8 1.0 %copy-done = bf16[128,2048]{1,0:T(8,128)(2,1)S(1)} copy-done((bf16[128,2048]{1,0:T(8,128)(2,1)S(1)}, bf16[128,2048]{1,0:T(8,128)(2,1)}, u32[]{:S(2)}) %copy-start) | copy-done | bytes 524312
  1.8 0.0 copy-start.1
  1.8 1.0 %copy-done.1 = bf16[128,2048]{1,0:T(8,128)(2,1)S(1)} copy-done((bf16[128,2048]{1,0:T(8,128)(2,1)S(1)}, bf16[128,2048]{1,0:T(8,128)(2,1)}, u32[]{:S(2)}) %copy-start.1) | copy-done | bytes 524312
  2.9 0.0 copy-start.2
  2.9 0.9 %copy-done.2 = bf16[128,512]{1,0:T(8,128)(2,1)S(1)} copy-done((bf16[128,512]{1,0:T(8,128)(2,1)S(1)}, bf16[128,512]{1,0:T(8,128)(2,1)}, u32[]{:S(2)}) %copy-start.2) | copy-done | bytes 131096
  3.8 59.3 %shard_map.46 = f32[128,512]{1,0:T(8,128)S(1)} custom-call(bf16[128,512]{1,0:T(8,128)(2,1)S(1)} %copy-done.2, bf16[128,2048]{1,0:T(8,128)(2,1)S(1)} %copy-done, s32[1,64,8]{2,1,0:T(8,128)S(1)} %copy.5.sel_ref, bf16[128,2048]{1,0:T(8,128)(2,1)S(1)} %copy-done.1), custom_call_target="tpu_custom_call" | custom-call | tf_op jit(solution)/shard_map/pallas_call | solution.py:306
  63.1 0.7 %copy.7 = f32[128,512]{1,0:T(8,128)} copy(f32[128,512]{1,0:T(8,128)S(1)} %shard_map.46) | data formatting | bytes 524288
Async XLA Ops:
  0.8 1.0 %copy-start = (bf16[128,2048]{1,0:T(8,128)(2,1)S(1)}, bf16[128,2048]{1,0:T(8,128)(2,1)}, u32[]{:S(2)}) copy-start(bf16[128,2048]{1,0:T(8,128)(2,1)} %kv_ref.1) | copy-start | bytes 1572868
  1.8 1.0 %copy-start.1 = (bf16[128,2048]{1,0:T(8,128)(2,1)S(1)}, bf16[128,2048]{1,0:T(8,128)(2,1)}, u32[]{:S(2)}) copy-start(bf16[128,2048]{1,0:T(8,128)(2,1)} %own_ref.1) | copy-start | bytes 1572868
  2.9 0.9 %copy-start.2 = (bf16[128,512]{1,0:T(8,128)(2,1)S(1)}, bf16[128,512]{1,0:T(8,128)(2,1)}, u32[]{:S(2)}) copy-start(bf16[128,512]{1,0:T(8,128)(2,1)} %q_ref.1) | copy-start | bytes 393220

commit v2 on v1

v2 whole, which is shorter than its diff:
```python
import math

import jax
import jax.numpy as jnp
from jax import lax
from jax.experimental import pallas as pl
from jax.experimental.pallas import tpu as pltpu
from jax.sharding import PartitionSpec as P

D = 128
R = 128
G = 8
NZ = 8
TOPK = 8
HEADS = 4
PAIRS = 16
PLANE = 16
FAR = -1e9
SCALE = math.log2(math.e) / math.sqrt(D)
MESH = pl.DeviceIdType.MESH
NT = (((1,), (1,)), ((), ()))


def remote(src, dst, send, recv, blk, hlp):
    return pltpu.make_async_remote_copy(
        src_ref=src, dst_ref=dst, send_sem=send, recv_sem=recv,
        device_id={"blk": blk, "help": hlp}, device_id_type=MESH,
    )


def kernel(
    q_ref, kv_ref, sel_ref, own_ref, out_ref,
    kvl, kvt, kvbuf, qbuf, sell, selv, sels, ownk, ownv, scores, part, stats, near, nstat,
    out_o, in_o, out_s, in_s,
    loc_sem, k_send, k_recv, f_send, f_recv,
    q_send, q_recv, s_send, s_recv, o_send, o_recv, t_send, t_recv,
):
    i = lax.axis_index("blk")
    j = lax.axis_index("help")
    g, u = i // 2, i % 2
    z, ylo = j // 2, j % 2
    me = 2 * g + ylo
    right = 2 * ((z + 1) % NZ) + ylo
    left = 2 * ((z + NZ - 1) % NZ) + ylo
    sib = 2 * g + (1 - u)

    def plane_of(t):
        return 2 * (t // 2) + u, 2 * z + t % 2

    barrier = pltpu.get_barrier_semaphore()

    def greet(b, h):
        pl.semaphore_signal(barrier, inc=1, device_id={"blk": b, "help": h}, device_id_type=MESH)

    lax.fori_loop(1, PLANE, lambda k, c: (greet(*plane_of((me + k) % PLANE)), c)[1], 0)
    lax.fori_loop(1, NZ, lambda k, c: (greet(i, 2 * ((z + k) % NZ) + ylo), c)[1], 0)
    greet(sib, j)

    gcol = pl.multiple_of(g * D, D)
    gval = pl.multiple_of(G * D + g * D, D)
    loads = [
        pltpu.make_async_copy(src, dst, loc_sem.at[n])
        for n, (src, dst) in enumerate((
            (kv_ref, kvl), (q_ref, qbuf.at[z]), (sel_ref.at[0], sell),
            (own_ref.at[:, pl.ds(gcol, D)], ownk), (own_ref.at[:, pl.ds(gval, D)], ownv),
        ))
    ]
    for copy in loads:
        copy.start()
    for copy in loads:
        copy.wait()
    for head in range(G):
        kvt[head, 0] = kvl[:, head * D : (head + 1) * D]
        kvt[head, 1] = jnp.transpose(kvl[:, (G + head) * D : (G + head + 1) * D])
    selv[z] = jnp.concatenate([sell[...], jnp.zeros((TOPK, D - sell.shape[1]), jnp.int32)], axis=1)
    kvbuf[i, ylo] = kvt[g]
    pl.semaphore_wait(barrier, PLANE - 1 + NZ - 1 + 1)

    def q_copy(way, s, half):
        block = (z - (s - 1)) % NZ if way == 0 else (z + (s - 1)) % NZ
        rows = pl.ds(half * (R // 2), R // 2)
        return remote(
            qbuf.at[block, rows, :], qbuf.at[block, rows, :],
            q_send.at[way, s - 1, half], q_recv.at[way, s - 1, half],
            i, right if way == 0 else left,
        )

    def q_halves(s):
        return [(w, h) for h in (0, 1) for w in (0, 1) if s < 4 or w == h]

    for w, h in q_halves(1):
        q_copy(w, 1, h).start()

    def kv_copy(k):
        t = (me + k) % PLANE
        b, h = plane_of(t)
        return remote(kvt.at[t // 2], kvbuf.at[i, ylo], k_send.at[k], k_recv.at[me], b, h)

    def forward(s):
        pair = 2 * (s // 2) + u
        slot = s % 2
        return remote(kvbuf.at[pair, slot], kvbuf.at[pair, slot], f_send.at[s], f_recv.at[s], sib, j)

    def s_copy(k):
        h = 2 * ((z + k) % NZ) + ylo
        return remote(selv.at[z], selv.at[z], s_send.at[k], s_recv.at[z], i, h)

    lax.fori_loop(1, PLANE, lambda k, c: (kv_copy(k).start(), c)[1], 0)
    lax.fori_loop(1, NZ, lambda k, c: (s_copy(k).start(), c)[1], 0)
    forward(me).start()

    causal = lax.broadcasted_iota(jnp.int32, (R, R), 0) <= lax.broadcasted_iota(jnp.int32, (R, R), 1)
    own_vt = jnp.transpose(ownv[...])
    for h in range(HEADS):
        s = lax.dot_general(
            ownk[...], qbuf[z, :, h * D : (h + 1) * D], NT, preferred_element_type=jnp.float32
        )
        s = jnp.where(causal, s, FAR)
        top = jnp.max(s, axis=0, keepdims=True)
        w = jnp.exp2((s - top) * SCALE)
        nstat[h : h + 1] = top
        nstat[HEADS + h : HEADS + h + 1] = jnp.sum(w, axis=0, keepdims=True)
        near[h] = jnp.dot(own_vt, w.astype(jnp.bfloat16), preferred_element_type=jnp.float32)

    def arrive(k, c):
        s = (me + PLANE - k) % PLANE
        pair = 2 * (s // 2) + u
        slot = s % 2
        remote(kvbuf.at[pair, slot], kvbuf.at[pair, slot], k_send.at[k], k_recv.at[s], sib, j).wait_recv()
        forward(s).start()
        return c

    def q_arrived(way, s, half):
        block = (z - s) % NZ if way == 0 else (z + s) % NZ
        rows = pl.ds(half * (R // 2), R // 2)
        remote(
            qbuf.at[block, rows, :], qbuf.at[block, rows, :], q_send.at[way, s - 1, half],
            q_recv.at[way, s - 1, half], i, right,
        ).wait_recv()

    for s, (lo, hi) in zip((1, 2, 3), ((1, 4), (4, 7), (7, 10))):
        lax.fori_loop(lo, hi, arrive, 0)
        ahead = q_halves(s + 1)
        for w, h in q_halves(s):
            q_arrived(w, s, h)
            if (w, h) in ahead:
                q_copy(w, s + 1, h).start()
    lax.fori_loop(10, PLANE, arrive, 0)
    for w, h in q_halves(4):
        q_arrived(w, 4, h)

    def picks_arrived(k, c):
        zs = (z + NZ - k) % NZ
        remote(selv.at[zs], selv.at[zs], s_send.at[k], s_recv.at[zs], i, right).wait_recv()
        return c

    lax.fori_loop(1, NZ, picks_arrived, 0)
    to_smem = pltpu.make_async_copy(selv, sels, loc_sem.at[0])
    to_smem.start()

    def from_sibling(s, c):
        pair = 2 * (s // 2) + (1 - u)
        slot = s % 2
        remote(kvbuf.at[pair, slot], kvbuf.at[pair, slot], f_send.at[s], f_recv.at[s], sib, j).wait_recv()
        return c

    lax.fori_loop(0, PLANE, from_sibling, 0)
    to_smem.wait()

    parity = z // (NZ // 2)
    lead = HEADS * i

    def attend(b):
        def first(h):
            q = qbuf[b, :, h * D : (h + 1) * D]
            top = jnp.full((1, R), 4 * FAR, jnp.float32)
            for t in range(TOPK):
                c = sels[b, t, lead + h]
                k = jnp.concatenate([kvbuf[c // 2, 0, 0], kvbuf[c // 2, 1, 0]], axis=0)
                s = lax.dot_general(k, q, NT, preferred_element_type=jnp.float32)
                scores[h % 2, t] = s
                bias = jnp.where(c % 2 == parity, 0.0, FAR)
                top = jnp.maximum(top, jnp.max(s, axis=0, keepdims=True) + bias)
            return top

        def second(h, top):
            total = jnp.zeros((1, R), jnp.float32)
            acc = jnp.zeros((D, R), jnp.float32)
            for t in range(TOPK):
                c = sels[b, t, lead + h]
                level = jnp.where(c % 2 == parity, top * SCALE, -FAR)
                w = jnp.exp2(scores[h % 2, t] * SCALE - level)
                total = total + jnp.sum(w, axis=0, keepdims=True)
                v = jnp.concatenate([kvbuf[c // 2, 0, 1], kvbuf[c // 2, 1, 1]], axis=1)
                acc = acc + jnp.dot(v, w.astype(jnp.bfloat16), preferred_element_type=jnp.float32)
            part[b, h] = acc
            stats[b, h : h + 1] = top
            stats[b, HEADS + h : HEADS + h + 1] = total

        top = first(0)
        for h in range(HEADS):
            after = first(h + 1) if h + 1 < HEADS else None
            second(h, top)
            top = after

    def merge(a, b):
        (ma, la, oa), (mb, lb, ob) = a, b
        m = jnp.maximum(ma, mb)
        fa, fb = jnp.exp2((ma - m) * SCALE), jnp.exp2((mb - m) * SCALE)
        return m, la * fa + lb * fb, oa * fa + ob * fb

    def mine(b, h):
        return stats[b, h : h + 1], stats[b, HEADS + h : HEADS + h + 1], part[b, h]

    def came(way, s, h):
        c, r = h // 2, h % 2
        return (
            in_s[way, s, c, r : r + 1], in_s[way, s, c, 2 + r : 3 + r],
            in_o[way, s, h].astype(jnp.float32),
        )

    def back(way, s, c):
        heads = pl.ds(2 * c, 2)
        hlp = jnp.where(way == 0, right, left)
        return (
            remote(out_o.at[way, s, heads], in_o.at[way, s, heads], o_send.at[way, s, c], o_recv.at[way, s, c], i, hlp),
            remote(out_s.at[way, s, c], in_s.at[way, s, c], t_send.at[way, s, c], t_recv.at[way, s, c], i, hlp),
        )

    def give(way, s, c, b):
        for h in (2 * c, 2 * c + 1):
            top, total, acc = mine(b, h)
            r = h % 2
            out_s[way, s, c, r : r + 1] = top
            out_s[way, s, c, 2 + r : 3 + r] = total
            out_o[way, s, h] = acc.astype(jnp.bfloat16)
        for copy in back(way, s, c):
            copy.start()

    def keep(b, h, state):
        stats[b, h : h + 1], stats[b, HEADS + h : HEADS + h + 1], part[b, h] = state

    def turn(n, carry):
        s = (n + 1) // 2
        way = (n + 1) % 2
        b = jnp.where(n == NZ - 1, z, jnp.where(way == 0, z + 4 - s, z + 4 + s) % NZ)
        attend(b)

        @pl.when(n == 0)
        def _():
            for c in (0, 1):
                give(c, 0, c, b)

        @pl.when((n > 0) & (n < NZ - 1))
        def _():
            for c in (0, 1):
                @pl.when((s >= 2) | (way == c))
                def _():
                    for copy in back(way, s - 1, c):
                        copy.wait_recv()
                    for h in (2 * c, 2 * c + 1):
                        keep(b, h, merge(mine(b, h), came(way, s - 1, h)))

                give(way, s, c, b)

        return carry

    lax.fori_loop(0, NZ, turn, 0)

    for h in range(HEADS):
        keep(z, h, merge(mine(z, h), (nstat[h : h + 1], nstat[HEADS + h : HEADS + h + 1], near[h])))
    for c in (0, 1):
        for way in (0, 1):
            for copy in back(way, 3, c):
                copy.wait_recv()
        for h in (2 * c, 2 * c + 1):
            state = merge(merge(mine(z, h), came(0, 3, h)), came(1, 3, h))
            out_ref[:, h * D : (h + 1) * D] = jnp.transpose(state[2] / state[1])

    for s in range(1, 5):
        for w, h in q_halves(s):
            q_copy(w, s, h).wait_send()
    lax.fori_loop(1, PLANE, lambda k, c: (kv_copy(k).wait_send(), c)[1], 0)
    lax.fori_loop(1, NZ, lambda k, c: (s_copy(k).wait_send(), c)[1], 0)
    lax.fori_loop(0, PLANE, lambda k, c: (forward(k).wait_send(), c)[1], 0)
    for s in range(4):
        for c in (0, 1):
            for way in (0, 1):
                if s >= 1 or c == way:
                    for copy in back(way, s, c):
                        copy.wait_send()


def local(queries, query_key_value, cached_key_value, selected):
    bf16, f32 = jnp.bfloat16, jnp.float32
    dma = pltpu.SemaphoreType.DMA
    hbm = pl.BlockSpec(memory_space=pl.ANY)
    return pl.pallas_call(
        kernel,
        out_shape=jax.ShapeDtypeStruct((R, HEADS * D), f32),
        in_specs=[hbm, hbm, hbm, hbm],
        out_specs=pl.BlockSpec(memory_space=pltpu.VMEM),
        scratch_shapes=[
            pltpu.VMEM((R, 2 * G * D), bf16),
            pltpu.VMEM((G, 2, R, D), bf16),
            pltpu.VMEM((PAIRS, 2, 2, R, D), bf16),
            pltpu.VMEM((NZ, R, HEADS * D), bf16),
            pltpu.VMEM((TOPK, PAIRS * HEADS), jnp.int32),
            pltpu.VMEM((NZ, TOPK, D), jnp.int32),
            pltpu.SMEM((NZ, TOPK, D), jnp.int32),
            pltpu.VMEM((R, D), bf16),
            pltpu.VMEM((R, D), bf16),
            pltpu.VMEM((2, TOPK, 2 * R, R), f32),
            pltpu.VMEM((NZ, HEADS, D, R), f32),
            pltpu.VMEM((NZ, 2 * HEADS, R), f32),
            pltpu.VMEM((HEADS, D, R), f32),
            pltpu.VMEM((2 * HEADS, R), f32),
            pltpu.VMEM((2, 4, HEADS, D, R), bf16),
            pltpu.VMEM((2, 4, HEADS, D, R), bf16),
            pltpu.VMEM((2, 4, 2, 8, R), f32),
            pltpu.VMEM((2, 4, 2, 8, R), f32),
            dma((5,)),
            dma((PLANE,)), dma((PLANE,)), dma((PLANE,)), dma((PLANE,)),
            dma((2, 4, 2)), dma((2, 4, 2)),
            dma((NZ,)), dma((NZ,)),
            dma((2, 4, 2)), dma((2, 4, 2)), dma((2, 4, 2)), dma((2, 4, 2)),
        ],
        compiler_params=pltpu.CompilerParams(
            collective_id=0, has_side_effects=True, vmem_limit_bytes=58 * 2**20
        ),
    )(queries, cached_key_value, jnp.transpose(selected, (0, 2, 1)), query_key_value)


def solution(mesh):
    in_specs = (P("help", "blk"), P("help", None), P(("blk", "help"), None), P("help", None, None))
    return jax.shard_map(
        local, mesh=mesh, in_specs=in_specs, out_specs=P("help", "blk"), check_vma=False
    )
```

time: 64 us -> 63.1 us (0.986)
  the two profiles are of different devices: /device:TPU:18 before, /device:TPU:26 now
where the time goes in v2:
time: 63.1 us; the launch traced here: 63 us
  Pallas kernels  61.3 us (97%)
  local copies, waits for them, and re-layouts  1.67 us (3%)
    pallas_call x1, Pallas kernels, local(): pl.pallas_call(kernel, out_shape=jax.ShapeDtypeStruct((R, HEADS * D), f32...  61.3 us
    unnamed x1, local copies, waits for them, and re-layouts  1.67 us

profile of v2, /device:TPU:26, one launch (start us, length us, event | category | flops | bytes accessed | tf_op | source)
XLA Modules:
  0.0 63.0 jit_solution(7153473378476639877)
XLA Ops:
  0.0 61.3 %shard_map.46 = f32[128,512]{1,0:T(8,128)} custom-call(bf16[128,512]{1,0:T(8,128)(2,1)} %q_ref.1, bf16[128,2048]{1,0:T(8,128)(2,1)} %kv_ref.1, s32[1,8,64]{2,1,0:T(8,128)} %bitcast.1, bf16[128,2048]{1,0:T(8,128)(2,1)} %own_ref.1), custom_call_target="tpu_custom_call" | custom-call | tf_op jit(solution)/shard_map/pallas_call | solution.py:298
  61.3 1.7 %copy.6 = f32[128,512]{1,0:T(8,128)} copy(f32[128,512]{1,0:T(8,128)} %shard_map.46) | data formatting | bytes 524288

commit v3 on v2

v3 whole, which is shorter than its diff:
```python
import math

import jax
import jax.numpy as jnp
from jax import lax
from jax.experimental import pallas as pl
from jax.experimental.pallas import tpu as pltpu
from jax.sharding import PartitionSpec as P

D = 128
R = 128
G = 8
NZ = 8
TOPK = 8
HEADS = 4
PAIRS = 16
PLANE = 16
MESSAGES = 7
FAR = -1e9
SCALE = math.log2(math.e) / math.sqrt(D)
MESH = pl.DeviceIdType.MESH
NT = (((1,), (1,)), ((), ()))


def remote(src, dst, send, recv, blk, hlp):
    return pltpu.make_async_remote_copy(
        src_ref=src, dst_ref=dst, send_sem=send, recv_sem=recv,
        device_id={"blk": blk, "help": hlp}, device_id_type=MESH,
    )


def kernel(
    q_ref, kv_ref, sel_ref, own_ref, out_ref,
    kvl, kvt, kbuf, vbuf, qbuf, sell, selv, sels, ownk, ownv, scores, part, stats, near, nstat,
    out_o, in_o, out_s, in_s,
    loc_sem, k_send, k_recv, f_send, f_recv,
    q_send, q_recv, s_send, s_recv, o_send, o_recv, t_send, t_recv,
):
    i = lax.axis_index("blk")
    j = lax.axis_index("help")
    g, u = i // 2, i % 2
    z, ylo = j // 2, j % 2
    me = 2 * g + ylo
    right = 2 * ((z + 1) % NZ) + ylo
    sib = 2 * g + (1 - u)

    def plane_of(t):
        return 2 * (t // 2) + u, 2 * z + t % 2

    barrier = pltpu.get_barrier_semaphore()

    def greet(b, h):
        pl.semaphore_signal(barrier, inc=1, device_id={"blk": b, "help": h}, device_id_type=MESH)

    lax.fori_loop(1, PLANE, lambda k, c: (greet(*plane_of((me + k) % PLANE)), c)[1], 0)
    lax.fori_loop(1, NZ, lambda k, c: (greet(i, 2 * ((z + k) % NZ) + ylo), c)[1], 0)
    greet(sib, j)

    gcol = pl.multiple_of(g * D, D)
    gval = pl.multiple_of(G * D + g * D, D)
    loads = [
        pltpu.make_async_copy(src, dst, loc_sem.at[n])
        for n, (src, dst) in enumerate((
            (kv_ref, kvl), (q_ref, qbuf.at[z]), (sel_ref.at[0], sell),
            (own_ref.at[:, pl.ds(gcol, D)], ownk), (own_ref.at[:, pl.ds(gval, D)], ownv),
        ))
    ]
    for copy in loads:
        copy.start()
    for copy in loads:
        copy.wait()
    for head in range(G):
        kvt[head, 0] = kvl[:, head * D : (head + 1) * D]
        kvt[head, 1] = jnp.transpose(kvl[:, (G + head) * D : (G + head + 1) * D])
    selv[z] = jnp.concatenate([sell[...], jnp.zeros((TOPK, D - sell.shape[1]), jnp.int32)], axis=1)
    kbuf[i, ylo] = kvt[g, 0]
    vbuf[i, ylo] = kvt[g, 1]
    pl.semaphore_wait(barrier, PLANE - 1 + NZ - 1 + 1)

    def at(d):
        return (z + d + NZ) % NZ

    def q_copy(n, half):
        src, hop = ((0, 1), (0, -1), (0, 2), (0, -2), (-2, 1), (2, -1), (-2, 2), (2, -2))[n]
        part_of = qbuf.at[at(src), pl.ds(half * (R // 2), R // 2), :]
        return remote(part_of, part_of, q_send.at[n, half], q_recv.at[n, half], i, 2 * at(hop) + ylo)

    def q_came(n, half):
        src = (-1, 1, -2, 2, -3, 3, -4, 4)[n]
        part_of = qbuf.at[at(src), pl.ds(half * (R // 2), R // 2), :]
        remote(part_of, part_of, q_send.at[n, half], q_recv.at[n, half], i, right).wait_recv()

    q_all = [(n, half) for half in (0, 1) for n in (2, 3, 0, 1)]
    q_far = [(n, half) for half in (0, 1) for n in (4, 6, 5, 7) if n < 6 or n == 6 + half]
    for n, half in q_all:
        q_copy(n, half).start()

    held = (kbuf, vbuf)

    def kv_copy(k, e):
        t = (me + k) % PLANE
        b, h = plane_of(t)
        return remote(kvt.at[t // 2, e], held[e].at[i, ylo], k_send.at[e, k], k_recv.at[e, me], b, h)

    def forward(s, e):
        block = held[e].at[2 * (s // 2) + u, s % 2]
        return remote(block, block, f_send.at[e, s], f_recv.at[e, s], sib, j)

    def s_copy(k):
        h = 2 * ((z + k) % NZ) + ylo
        return remote(selv.at[z], selv.at[z], s_send.at[k], s_recv.at[z], i, h)

    lax.fori_loop(1, PLANE, lambda k, c: (kv_copy(k, 0).start(), c)[1], 0)
    lax.fori_loop(1, NZ, lambda k, c: (s_copy(k).start(), c)[1], 0)
    lax.fori_loop(1, PLANE, lambda k, c: (kv_copy(k, 1).start(), c)[1], 0)
    for e in (0, 1):
        forward(me, e).start()

    causal = lax.broadcasted_iota(jnp.int32, (R, R), 0) <= lax.broadcasted_iota(jnp.int32, (R, R), 1)
    own_vt = jnp.transpose(ownv[...])
    for h in range(HEADS):
        s = lax.dot_general(
            ownk[...], qbuf[z, :, h * D : (h + 1) * D], NT, preferred_element_type=jnp.float32
        )
        s = jnp.where(causal, s, FAR)
        top = jnp.max(s, axis=0, keepdims=True)
        w = jnp.exp2((s - top) * SCALE)
        nstat[h, 0:1] = top
        nstat[h, 1:2] = jnp.sum(w, axis=0, keepdims=True)
        near[h] = jnp.dot(own_vt, w.astype(jnp.bfloat16), preferred_element_type=jnp.float32)

    for half in (0, 1):
        for n in (2, 3):
            q_came(n, half)
            for m, other in q_far:
                if other == half and m % 2 == n % 2:
                    q_copy(m, half).start()

    def arrive(e):
        def one(k, c):
            s = (me + PLANE - k) % PLANE
            block = held[e].at[2 * (s // 2) + u, s % 2]
            remote(block, block, k_send.at[e, k], k_recv.at[e, s], sib, j).wait_recv()
            forward(s, e).start()
            return c

        lax.fori_loop(1, PLANE, one, 0)

    def from_sibling(e):
        def one(s, c):
            block = held[e].at[2 * (s // 2) + (1 - u), s % 2]
            remote(block, block, f_send.at[e, s], f_recv.at[e, s], sib, j).wait_recv()
            return c

        lax.fori_loop(0, PLANE, one, 0)

    def picks_came(k, c):
        zs = (z + NZ - k) % NZ
        remote(selv.at[zs], selv.at[zs], s_send.at[k], s_recv.at[zs], i, right).wait_recv()
        return c

    lax.fori_loop(1, NZ, picks_came, 0)
    to_smem = pltpu.make_async_copy(selv, sels, loc_sem.at[0])
    to_smem.start()
    arrive(0)
    for n, half in q_all + q_far:
        if n not in (2, 3):
            q_came(n, half)
    to_smem.wait()
    from_sibling(0)

    parity = z // (NZ // 2)
    lead = HEADS * i

    def score(b, carry):
        for h in range(HEADS):
            q = qbuf[b, :, h * D : (h + 1) * D]
            top = jnp.full((1, R), 4 * FAR, jnp.float32)
            for t in range(TOPK):
                c = sels[b, t, lead + h]
                k = kbuf[c // 2].reshape(2 * R, D)
                s = lax.dot_general(k, q, NT, preferred_element_type=jnp.float32)
                scores[b, h, t] = s
                bias = jnp.where(c % 2 == parity, 0.0, FAR)
                top = jnp.maximum(top, jnp.max(s, axis=0, keepdims=True) + bias)
            stats[b, h, 0:1] = top
        return carry

    lax.fori_loop(0, NZ, score, 0)
    arrive(1)
    from_sibling(1)

    def attend(b, h):
        top = stats[b, h, 0:1]
        total = jnp.zeros((1, R), jnp.float32)
        acc = jnp.zeros((D, R), jnp.float32)
        for t in range(TOPK):
            c = sels[b, t, lead + h]
            level = jnp.where(c % 2 == parity, top * SCALE, -FAR)
            w = jnp.exp2(scores[b, h, t] * SCALE - level)
            total = total + jnp.sum(w, axis=0, keepdims=True)
            v = jnp.concatenate([vbuf[c // 2, 0], vbuf[c // 2, 1]], axis=1)
            acc = acc + jnp.dot(v, w.astype(jnp.bfloat16), preferred_element_type=jnp.float32)
        part[b, h] = acc
        stats[b, h, 1:2] = total

    def merge(a, b):
        (ma, la, oa), (mb, lb, ob) = a, b
        m = jnp.maximum(ma, mb)
        fa, fb = jnp.exp2((ma - m) * SCALE), jnp.exp2((mb - m) * SCALE)
        return m, la * fa + lb * fb, oa * fa + ob * fb

    def mine(b, h):
        return stats[b, h, 0:1], stats[b, h, 1:2], part[b, h]

    def came(n, h):
        return in_s[n, h, 0:1], in_s[n, h, 1:2], in_o[n, h].astype(jnp.float32)

    def back(n, c, hop):
        heads = pl.ds(2 * c, 2)
        hlp = 2 * at(hop) + ylo
        return (
            remote(out_o.at[n, heads], in_o.at[n, heads], o_send.at[n, c], o_recv.at[n, c], i, hlp),
            remote(out_s.at[n, heads], in_s.at[n, heads], t_send.at[n, c], t_recv.at[n, c], i, hlp),
        )

    def landed(n, c):
        for copy in back(n, c, 1):
            copy.wait_recv()

    def give(n, c, hop, b, others=()):
        for e in (0, 1):
            h = 2 * c + e
            state = mine(b, h)
            for other in others:
                state = merge(state, came(other, h))
            out_s[n, h, 0:1] = state[0]
            out_s[n, h, 1:2] = state[1]
            out_o[n, h] = state[2].astype(jnp.bfloat16)
        for copy in back(n, c, hop):
            copy.start()

    order = (4, 3, -3, 1, 2, -2, -1, 0)
    messages = {1: (1, 1), 2: (2, -1), 3: (3, 1), 4: (5, 2), 5: (6, -2), 6: (4, -1)}

    def turn(m, carry):
        n, c = m // 2, m % 2
        b = z
        for at_turn, d in enumerate(order):
            b = jnp.where(n == at_turn, at(d), b)
        for e in (0, 1):
            attend(b, 2 * c + e)
        for side in (0, 1):
            @pl.when((n == 0) & (c == side))
            def _(side=side):
                give(0, side, 2 - 4 * side, b)

        for at_turn, (message, hop) in messages.items():
            @pl.when(n == at_turn)
            def _(message=message, hop=hop):
                if message >= 5:
                    side = message - 5
                    landed(message - 4, c)

                    @pl.when(c == side)
                    def _():
                        landed(0, side)
                        give(message, side, hop, b, (message - 4, 0))

                    @pl.when(c != side)
                    def _():
                        give(message, 1 - side, hop, b, (message - 4,))
                else:
                    give(message, c, hop, b)

        return carry

    lax.fori_loop(0, 2 * NZ, turn, 0)

    for c in (0, 1):
        for n in (3, 5, 6, 4):
            landed(n, c)
        for h in (2 * c, 2 * c + 1):
            state = merge(mine(z, h), (nstat[h, 0:1], nstat[h, 1:2], near[h]))
            for n in (3, 5, 6, 4):
                state = merge(state, came(n, h))
            out_ref[:, h * D : (h + 1) * D] = jnp.transpose(state[2] / state[1])

    for n, half in q_all + q_far:
        q_copy(n, half).wait_send()
    for e in (0, 1):
        lax.fori_loop(1, PLANE, lambda k, c: (kv_copy(k, e).wait_send(), c)[1], 0)
        lax.fori_loop(0, PLANE, lambda k, c: (forward(k, e).wait_send(), c)[1], 0)
    lax.fori_loop(1, NZ, lambda k, c: (s_copy(k).wait_send(), c)[1], 0)
    for c in (0, 1):
        for n in range(MESSAGES):
            for copy in back(n, c, 1):
                copy.wait_send()


def local(queries, query_key_value, cached_key_value, selected):
    bf16, f32 = jnp.bfloat16, jnp.float32
    dma = pltpu.SemaphoreType.DMA
    hbm = pl.BlockSpec(memory_space=pl.ANY)
    return pl.pallas_call(
        kernel,
        out_shape=jax.ShapeDtypeStruct((R, HEADS * D), f32),
        in_specs=[hbm, hbm, hbm, hbm],
        out_specs=pl.BlockSpec(memory_space=pltpu.VMEM),
        scratch_shapes=[
            pltpu.VMEM((R, 2 * G * D), bf16),
            pltpu.VMEM((G, 2, R, D), bf16),
            pltpu.VMEM((PAIRS, 2, R, D), bf16),
            pltpu.VMEM((PAIRS, 2, D, R), bf16),
            pltpu.VMEM((NZ, R, HEADS * D), bf16),
            pltpu.VMEM((TOPK, PAIRS * HEADS), jnp.int32),
            pltpu.VMEM((NZ, TOPK, D), jnp.int32),
            pltpu.SMEM((NZ, TOPK, D), jnp.int32),
            pltpu.VMEM((R, D), bf16),
            pltpu.VMEM((R, D), bf16),
            pltpu.VMEM((NZ, HEADS, TOPK, 2 * R, R), f32),
            pltpu.VMEM((NZ, HEADS, D, R), f32),
            pltpu.VMEM((NZ, HEADS, 8, R), f32),
            pltpu.VMEM((HEADS, D, R), f32),
            pltpu.VMEM((HEADS, 8, R), f32),
            pltpu.VMEM((MESSAGES, HEADS, D, R), bf16),
            pltpu.VMEM((MESSAGES, HEADS, D, R), bf16),
            pltpu.VMEM((MESSAGES, HEADS, 8, R), f32),
            pltpu.VMEM((MESSAGES, HEADS, 8, R), f32),
            dma((5,)),
            dma((2, PLANE)), dma((2, PLANE)), dma((2, PLANE)), dma((2, PLANE)),
            dma((8, 2)), dma((8, 2)),
            dma((NZ,)), dma((NZ,)),
            dma((MESSAGES, 2)), dma((MESSAGES, 2)), dma((MESSAGES, 2)), dma((MESSAGES, 2)),
        ],
        compiler_params=pltpu.CompilerParams(
            collective_id=0, has_side_effects=True, vmem_limit_bytes=58 * 2**20
        ),
    )(queries, cached_key_value, jnp.transpose(selected, (0, 2, 1)), query_key_value)


def solution(mesh):
    in_specs = (P("help", "blk"), P("help", None), P(("blk", "help"), None), P("help", None, None))
    return jax.shard_map(
        local, mesh=mesh, in_specs=in_specs, out_specs=P("help", "blk"), check_vma=False
    )
```

time: 63.1 us -> 61.6 us (0.976)
  the two profiles are of different devices: /device:TPU:26 before, /device:TPU:1 now
where the time goes in v3:
time: 61.6 us; the launch traced here: 61.5 us
  Pallas kernels  59.8 us (97%)
  local copies, waits for them, and re-layouts  1.67 us (3%)
    pallas_call x1, Pallas kernels, local(): pl.pallas_call(kernel, out_shape=jax.ShapeDtypeStruct((R, HEADS * D), f32...  59.8 us
    unnamed x1, local copies, waits for them, and re-layouts  1.67 us

profile of v3, /device:TPU:1, one launch (start us, length us, event | category | flops | bytes accessed | tf_op | source)
XLA Modules:
  0.0 61.5 jit_solution(2012281300327127584)
XLA Ops:
  0.0 59.8 %shard_map.46 = f32[128,512]{1,0:T(8,128)} custom-call(bf16[128,512]{1,0:T(8,128)(2,1)} %q_ref.1, bf16[128,2048]{1,0:T(8,128)(2,1)} %kv_ref.1, s32[1,8,64]{2,1,0:T(8,128)} %bitcast.1, bf16[128,2048]{1,0:T(8,128)(2,1)} %own_ref.1), custom_call_target="tpu_custom_call" | custom-call | tf_op jit(solution)/shard_map/pallas_call | solution.py:305
  59.8 1.7 %copy.6 = f32[128,512]{1,0:T(8,128)} copy(f32[128,512]{1,0:T(8,128)} %shard_map.46) | data formatting | bytes 524288

commit v4 on v3

--- a/solution.py
+++ b/solution.py
@@ -15,7 +15,7 @@
 HEADS = 4
 PAIRS = 16
 PLANE = 16
-MESSAGES = 7
+PIECES = 4
 FAR = -1e9
 SCALE = math.log2(math.e) / math.sqrt(D)
 MESH = pl.DeviceIdType.MESH
@@ -80,20 +80,30 @@
     def at(d):
         return (z + d + NZ) % NZ
 
-    def q_copy(n, half):
-        src, hop = ((0, 1), (0, -1), (0, 2), (0, -2), (-2, 1), (2, -1), (-2, 2), (2, -2))[n]
-        part_of = qbuf.at[at(src), pl.ds(half * (R // 2), R // 2), :]
-        return remote(part_of, part_of, q_send.at[n, half], q_recv.at[n, half], i, 2 * at(hop) + ylo)
-
-    def q_came(n, half):
-        src = (-1, 1, -2, 2, -3, 3, -4, 4)[n]
-        part_of = qbuf.at[at(src), pl.ds(half * (R // 2), R // 2), :]
-        remote(part_of, part_of, q_send.at[n, half], q_recv.at[n, half], i, right).wait_recv()
-
-    q_all = [(n, half) for half in (0, 1) for n in (2, 3, 0, 1)]
-    q_far = [(n, half) for half in (0, 1) for n in (4, 6, 5, 7) if n < 6 or n == 6 + half]
-    for n, half in q_all:
-        q_copy(n, half).start()
+    def q_piece(block, p):
+        return qbuf.at[at(block), pl.ds(p * (R // PIECES), R // PIECES), :]
+
+    def q_copy(way, s, p):
+        part_of = q_piece((s - 1) * (2 * way - 1), p)
+        return remote(
+            part_of, part_of, q_send.at[way, s - 1, p], q_recv.at[way, s - 1, p], i, 2 * at(1 - 2 * way) + ylo
+        )
+
+    def q_came(way, s, p):
+        part_of = q_piece(s * (2 * way - 1), p)
+        remote(part_of, part_of, q_send.at[way, s - 1, p], q_recv.at[way, s - 1, p], i, right).wait_recv()
+
+    def q_steps(s):
+        return [(w, p) for p in range(PIECES) for w in (0, 1) if s < 4 or p // (PIECES // 2) == w]
+
+    def q_pass_on(s):
+        for w, p in q_steps(s):
+            q_came(w, s, p)
+            if (w, p) in q_steps(s + 1):
+                q_copy(w, s + 1, p).start()
+
+    for w, p in q_steps(1):
+        q_copy(w, 1, p).start()
 
     held = (kbuf, vbuf)
 
@@ -129,13 +139,6 @@
         nstat[h, 1:2] = jnp.sum(w, axis=0, keepdims=True)
         near[h] = jnp.dot(own_vt, w.astype(jnp.bfloat16), preferred_element_type=jnp.float32)
 
-    for half in (0, 1):
-        for n in (2, 3):
-            q_came(n, half)
-            for m, other in q_far:
-                if other == half and m % 2 == n % 2:
-                    q_copy(m, half).start()
-
     def arrive(e):
         def one(k, c):
             s = (me + PLANE - k) % PLANE
@@ -159,13 +162,13 @@
         remote(selv.at[zs], selv.at[zs], s_send.at[k], s_recv.at[zs], i, right).wait_recv()
         return c
 
+    q_pass_on(1)
     lax.fori_loop(1, NZ, picks_came, 0)
     to_smem = pltpu.make_async_copy(selv, sels, loc_sem.at[0])
     to_smem.start()
+    q_pass_on(2)
     arrive(0)
-    for n, half in q_all + q_far:
-        if n not in (2, 3):
-            q_came(n, half)
+    q_pass_on(3)
     to_smem.wait()
     from_sibling(0)
 
@@ -186,8 +189,11 @@
             stats[b, h, 0:1] = top
         return carry
 
-    lax.fori_loop(0, NZ, score, 0)
+    lax.fori_loop(0, NZ - 1, lambda n, c: score((z + 5 + n) % NZ, c), 0)
     arrive(1)
+    for w, p in q_steps(4):
+        q_came(w, 4, p)
+    score(at(4), 0)
     from_sibling(1)
 
     def attend(b, h):
@@ -213,89 +219,75 @@
     def mine(b, h):
         return stats[b, h, 0:1], stats[b, h, 1:2], part[b, h]
 
-    def came(n, h):
-        return in_s[n, h, 0:1], in_s[n, h, 1:2], in_o[n, h].astype(jnp.float32)
-
-    def back(n, c, hop):
-        heads = pl.ds(2 * c, 2)
-        hlp = 2 * at(hop) + ylo
+    def came(way, s, h):
+        return in_s[way, s, h, 0:1], in_s[way, s, h, 1:2], in_o[way, s, h].astype(jnp.float32)
+
+    def back(way, s, h):
+        hlp = 2 * ((z + 1 + (NZ - 2) * way) % NZ) + ylo
         return (
-            remote(out_o.at[n, heads], in_o.at[n, heads], o_send.at[n, c], o_recv.at[n, c], i, hlp),
-            remote(out_s.at[n, heads], in_s.at[n, heads], t_send.at[n, c], t_recv.at[n, c], i, hlp),
+            remote(out_o.at[way, s, h], in_o.at[way, s, h], o_send.at[way, s, h], o_recv.at[way, s, h], i, hlp),
+            remote(out_s.at[way, s, h], in_s.at[way, s, h], t_send.at[way, s, h], t_recv.at[way, s, h], i, hlp),
         )
 
-    def landed(n, c):
-        for copy in back(n, c, 1):
+    def landed(way, s, h):
+        for copy in back(way, s, h):
             copy.wait_recv()
 
-    def give(n, c, hop, b, others=()):
-        for e in (0, 1):
-            h = 2 * c + e
-            state = mine(b, h)
-            for other in others:
-                state = merge(state, came(other, h))
-            out_s[n, h, 0:1] = state[0]
-            out_s[n, h, 1:2] = state[1]
-            out_o[n, h] = state[2].astype(jnp.bfloat16)
-        for copy in back(n, c, hop):
+    def give(way, s, h, state):
+        out_s[way, s, h, 0:1] = state[0]
+        out_s[way, s, h, 1:2] = state[1]
+        out_o[way, s, h] = state[2].astype(jnp.bfloat16)
+        for copy in back(way, s, h):
             copy.start()
-
-    order = (4, 3, -3, 1, 2, -2, -1, 0)
-    messages = {1: (1, 1), 2: (2, -1), 3: (3, 1), 4: (5, 2), 5: (6, -2), 6: (4, -1)}
 
     def turn(m, carry):
         n, c = m // 2, m % 2
-        b = z
-        for at_turn, d in enumerate(order):
-            b = jnp.where(n == at_turn, at(d), b)
+        s = (n + 1) // 2
+        way = (n + 1) % 2
+        b = jnp.where(n == NZ - 1, z, jnp.where(way == 0, z + 4 - s, z + 4 + s) % NZ)
         for e in (0, 1):
             attend(b, 2 * c + e)
-        for side in (0, 1):
-            @pl.when((n == 0) & (c == side))
-            def _(side=side):
-                give(0, side, 2 - 4 * side, b)
-
-        for at_turn, (message, hop) in messages.items():
-            @pl.when(n == at_turn)
-            def _(message=message, hop=hop):
-                if message >= 5:
-                    side = message - 5
-                    landed(message - 4, c)
-
-                    @pl.when(c == side)
-                    def _():
-                        landed(0, side)
-                        give(message, side, hop, b, (message - 4, 0))
-
-                    @pl.when(c != side)
-                    def _():
-                        give(message, 1 - side, hop, b, (message - 4,))
-                else:
-                    give(message, c, hop, b)
+
+        @pl.when(n == 0)
+        def _():
+            for e in (0, 1):
+                give(c, 0, 2 * c + e, mine(b, 2 * c + e))
+
+        @pl.when(((n == 1) | (n == 2)) & (c != way))
+        def _():
+            for e in (0, 1):
+                give(way, s, 2 * c + e, mine(b, 2 * c + e))
+
+        @pl.when((n < NZ - 1) & ((n > 2) | ((n > 0) & (c == way))))
+        def _():
+            for e in (0, 1):
+                landed(way, s - 1, 2 * c + e)
+                give(way, s, 2 * c + e, merge(mine(b, 2 * c + e), came(way, s - 1, 2 * c + e)))
 
         return carry
 
     lax.fori_loop(0, 2 * NZ, turn, 0)
 
-    for c in (0, 1):
-        for n in (3, 5, 6, 4):
-            landed(n, c)
-        for h in (2 * c, 2 * c + 1):
-            state = merge(mine(z, h), (nstat[h, 0:1], nstat[h, 1:2], near[h]))
-            for n in (3, 5, 6, 4):
-                state = merge(state, came(n, h))
-            out_ref[:, h * D : (h + 1) * D] = jnp.transpose(state[2] / state[1])
-
-    for n, half in q_all + q_far:
-        q_copy(n, half).wait_send()
+    for h in range(HEADS):
+        state = merge(mine(z, h), (nstat[h, 0:1], nstat[h, 1:2], near[h]))
+        for way in (0, 1):
+            landed(way, 3, h)
+            state = merge(state, came(way, 3, h))
+        out_ref[:, h * D : (h + 1) * D] = jnp.transpose(state[2] / state[1])
+
+    for s in range(1, 5):
+        for w, p in q_steps(s):
+            q_copy(w, s, p).wait_send()
     for e in (0, 1):
         lax.fori_loop(1, PLANE, lambda k, c: (kv_copy(k, e).wait_send(), c)[1], 0)
         lax.fori_loop(0, PLANE, lambda k, c: (forward(k, e).wait_send(), c)[1], 0)
     lax.fori_loop(1, NZ, lambda k, c: (s_copy(k).wait_send(), c)[1], 0)
-    for c in (0, 1):
-        for n in range(MESSAGES):
-            for copy in back(n, c, 1):
-                copy.wait_send()
+    for s in range(4):
+        for way in (0, 1):
+            for h in range(HEADS):
+                if s > 0 or h // 2 == way:
+                    for copy in back(way, s, h):
+                        copy.wait_send()
 
 
 def local(queries, query_key_value, cached_key_value, selected):
@@ -323,15 +315,15 @@
             pltpu.VMEM((NZ, HEADS, 8, R), f32),
             pltpu.VMEM((HEADS, D, R), f32),
             pltpu.VMEM((HEADS, 8, R), f32),
-            pltpu.VMEM((MESSAGES, HEADS, D, R), bf16),
-            pltpu.VMEM((MESSAGES, HEADS, D, R), bf16),
-            pltpu.VMEM((MESSAGES, HEADS, 8, R), f32),
-            pltpu.VMEM((MESSAGES, HEADS, 8, R), f32),
+            pltpu.VMEM((2, 4, HEADS, D, R), bf16),
+            pltpu.VMEM((2, 4, HEADS, D, R), bf16),
+            pltpu.VMEM((2, 4, HEADS, 8, R), f32),
+            pltpu.VMEM((2, 4, HEADS, 8, R), f32),
             dma((5,)),
             dma((2, PLANE)), dma((2, PLANE)), dma((2, PLANE)), dma((2, PLANE)),
-            dma((8, 2)), dma((8, 2)),
+            dma((2, 4, PIECES)), dma((2, 4, PIECES)),
             dma((NZ,)), dma((NZ,)),
-            dma((MESSAGES, 2)), dma((MESSAGES, 2)), dma((MESSAGES, 2)), dma((MESSAGES, 2)),
+            dma((2, 4, HEADS)), dma((2, 4, HEADS)), dma((2, 4, HEADS)), dma((2, 4, HEADS)),
         ],
         compiler_params=pltpu.CompilerParams(
             collective_id=0, has_side_effects=True, vmem_limit_bytes=58 * 2**20

time: 61.6 us -> 54.4 us (0.88)
  Pallas kernels: 59.8 us -> 52.6 us
    pallas_call x1, Pallas kernels: 59.8 us -> 52.6 us  [local(): pl.pallas_call(kernel, out_shape=jax.ShapeDtypeStruct((R, HEADS * D), f32...]
where the time goes in v4:
time: 54.4 us; the launch traced here: 54.3 us
  Pallas kernels  52.6 us (97%)
  local copies, waits for them, and re-layouts  1.67 us (3%)
    pallas_call x1, Pallas kernels, local(): pl.pallas_call(kernel, out_shape=jax.ShapeDtypeStruct((R, HEADS * D), f32...  52.6 us
    unnamed x1, local copies, waits for them, and re-layouts  1.67 us

profile of v4, /device:TPU:1, one launch (start us, length us, event | category | flops | bytes accessed | tf_op | source)
XLA Modules:
  0.0 54.3 jit_solution(651490001578280077)
XLA Ops:
  0.0 52.6 %shard_map.46 = f32[128,512]{1,0:T(8,128)} custom-call(bf16[128,512]{1,0:T(8,128)(2,1)} %q_ref.1, bf16[128,2048]{1,0:T(8,128)(2,1)} %kv_ref.1, s32[1,8,64]{2,1,0:T(8,128)} %bitcast.1, bf16[128,2048]{1,0:T(8,128)(2,1)} %own_ref.1), custom_call_target="tpu_custom_call" | custom-call | tf_op jit(solution)/shard_map/pallas_call | solution.py:297
  52.6 1.7 %copy.6 = f32[128,512]{1,0:T(8,128)} copy(f32[128,512]{1,0:T(8,128)} %shard_map.46) | data formatting | bytes 524288

commit v5 on v4

--- a/solution.py
+++ b/solution.py
@@ -31,7 +31,7 @@
 
 def kernel(
     q_ref, kv_ref, sel_ref, own_ref, out_ref,
-    kvl, kvt, kbuf, vbuf, qbuf, sell, selv, sels, ownk, ownv, scores, part, stats, near, nstat,
+    kvl, vts, kbuf, vbuf, qbuf, sell, selv, sels, ownk, ownv, scores, part, stats, near, nstat,
     out_o, in_o, out_s, in_s,
     loc_sem, k_send, k_recv, f_send, f_recv,
     q_send, q_recv, s_send, s_recv, o_send, o_recv, t_send, t_recv,
@@ -67,14 +67,6 @@
     ]
     for copy in loads:
         copy.start()
-    for copy in loads:
-        copy.wait()
-    for head in range(G):
-        kvt[head, 0] = kvl[:, head * D : (head + 1) * D]
-        kvt[head, 1] = jnp.transpose(kvl[:, (G + head) * D : (G + head + 1) * D])
-    selv[z] = jnp.concatenate([sell[...], jnp.zeros((TOPK, D - sell.shape[1]), jnp.int32)], axis=1)
-    kbuf[i, ylo] = kvt[g, 0]
-    vbuf[i, ylo] = kvt[g, 1]
     pl.semaphore_wait(barrier, PLANE - 1 + NZ - 1 + 1)
 
     def at(d):
@@ -84,9 +76,12 @@
         return qbuf.at[at(block), pl.ds(p * (R // PIECES), R // PIECES), :]
 
     def q_copy(way, s, p):
-        part_of = q_piece((s - 1) * (2 * way - 1), p)
+        hop = 2 if s == 4 else 1
+        part_of = q_piece((s - hop) * (2 * way - 1), p)
+        src = q_ref.at[pl.ds(p * (R // PIECES), R // PIECES), :] if s == 1 else part_of
         return remote(
-            part_of, part_of, q_send.at[way, s - 1, p], q_recv.at[way, s - 1, p], i, 2 * at(1 - 2 * way) + ylo
+            src, part_of, q_send.at[way, s - 1, p], q_recv.at[way, s - 1, p],
+            i, 2 * at(hop * (1 - 2 * way)) + ylo,
         )
 
     def q_came(way, s, p):
@@ -99,18 +94,22 @@
     def q_pass_on(s):
         for w, p in q_steps(s):
             q_came(w, s, p)
-            if (w, p) in q_steps(s + 1):
-                q_copy(w, s + 1, p).start()
+            if s == 2 and (w, p) in q_steps(4):
+                q_copy(w, 4, p).start()
+            q_copy(w, s + 1, p).start()
 
     for w, p in q_steps(1):
         q_copy(w, 1, p).start()
+    for copy in loads:
+        copy.wait()
 
     held = (kbuf, vbuf)
 
     def kv_copy(k, e):
         t = (me + k) % PLANE
         b, h = plane_of(t)
-        return remote(kvt.at[t // 2, e], held[e].at[i, ylo], k_send.at[e, k], k_recv.at[e, me], b, h)
+        src = vts.at[t // 2] if e else kvl.at[:, pl.ds(pl.multiple_of((t // 2) * D, D), D)]
+        return remote(src, held[e].at[i, ylo], k_send.at[e, k], k_recv.at[e, me], b, h)
 
     def forward(s, e):
         block = held[e].at[2 * (s // 2) + u, s % 2]
@@ -121,10 +120,45 @@
         return remote(selv.at[z], selv.at[z], s_send.at[k], s_recv.at[z], i, h)
 
     lax.fori_loop(1, PLANE, lambda k, c: (kv_copy(k, 0).start(), c)[1], 0)
+    selv[z] = jnp.concatenate([sell[...], jnp.zeros((TOPK, D - sell.shape[1]), jnp.int32)], axis=1)
     lax.fori_loop(1, NZ, lambda k, c: (s_copy(k).start(), c)[1], 0)
+    kbuf[i, ylo] = kvl[:, pl.ds(gcol, D)]
+    forward(me, 0).start()
+    for head in range(G):
+        vts[head] = jnp.transpose(kvl[:, (G + head) * D : (G + head + 1) * D])
+    vbuf[i, ylo] = vts[g]
+
+    def arrive(e):
+        def one(k, c):
+            s = (me + PLANE - k) % PLANE
+            block = held[e].at[2 * (s // 2) + u, s % 2]
+            remote(block, block, k_send.at[e, k], k_recv.at[e, s], sib, j).wait_recv()
+            forward(s, e).start()
+            return c
+
+        lax.fori_loop(1, PLANE, one, 0)
+
+    def from_sibling(e):
+        def one(s, c):
+            block = held[e].at[2 * (s // 2) + (1 - u), s % 2]
+            remote(block, block, f_send.at[e, s], f_recv.at[e, s], sib, j).wait_recv()
+            return c
+
+        lax.fori_loop(0, PLANE, one, 0)
+
+    def picks_came(k, c):
+        zs = (z + NZ - k) % NZ
+        remote(selv.at[zs], selv.at[zs], s_send.at[k], s_recv.at[zs], i, right).wait_recv()
+        return c
+
+    q_pass_on(1)
     lax.fori_loop(1, PLANE, lambda k, c: (kv_copy(k, 1).start(), c)[1], 0)
-    for e in (0, 1):
-        forward(me, e).start()
+    forward(me, 1).start()
+    lax.fori_loop(1, NZ, picks_came, 0)
+    to_smem = pltpu.make_async_copy(selv, sels, loc_sem.at[0])
+    to_smem.start()
+    q_pass_on(2)
+    arrive(0)
 
     causal = lax.broadcasted_iota(jnp.int32, (R, R), 0) <= lax.broadcasted_iota(jnp.int32, (R, R), 1)
     own_vt = jnp.transpose(ownv[...])
@@ -139,36 +173,6 @@
         nstat[h, 1:2] = jnp.sum(w, axis=0, keepdims=True)
         near[h] = jnp.dot(own_vt, w.astype(jnp.bfloat16), preferred_element_type=jnp.float32)
 
-    def arrive(e):
-        def one(k, c):
-            s = (me + PLANE - k) % PLANE
-            block = held[e].at[2 * (s // 2) + u, s % 2]
-            remote(block, block, k_send.at[e, k], k_recv.at[e, s], sib, j).wait_recv()
-            forward(s, e).start()
-            return c
-
-        lax.fori_loop(1, PLANE, one, 0)
-
-    def from_sibling(e):
-        def one(s, c):
-            block = held[e].at[2 * (s // 2) + (1 - u), s % 2]
-            remote(block, block, f_send.at[e, s], f_recv.at[e, s], sib, j).wait_recv()
-            return c
-
-        lax.fori_loop(0, PLANE, one, 0)
-
-    def picks_came(k, c):
-        zs = (z + NZ - k) % NZ
-        remote(selv.at[zs], selv.at[zs], s_send.at[k], s_recv.at[zs], i, right).wait_recv()
-        return c
-
-    q_pass_on(1)
-    lax.fori_loop(1, NZ, picks_came, 0)
-    to_smem = pltpu.make_async_copy(selv, sels, loc_sem.at[0])
-    to_smem.start()
-    q_pass_on(2)
-    arrive(0)
-    q_pass_on(3)
     to_smem.wait()
     from_sibling(0)
 
@@ -189,11 +193,12 @@
             stats[b, h, 0:1] = top
         return carry
 
-    lax.fori_loop(0, NZ - 1, lambda n, c: score((z + 5 + n) % NZ, c), 0)
+    lax.fori_loop(0, NZ - 3, lambda n, c: score((z + 6 + n) % NZ, c), 0)
+    for s in (3, 4):
+        for w, p in q_steps(s):
+            q_came(w, s, p)
     arrive(1)
-    for w, p in q_steps(4):
-        q_came(w, 4, p)
-    score(at(4), 0)
+    lax.fori_loop(0, 3, lambda n, c: score((z + 3 + n) % NZ, c), 0)
     from_sibling(1)
 
     def attend(b, h):
@@ -205,8 +210,11 @@
             level = jnp.where(c % 2 == parity, top * SCALE, -FAR)
             w = jnp.exp2(scores[b, h, t] * SCALE - level)
             total = total + jnp.sum(w, axis=0, keepdims=True)
-            v = jnp.concatenate([vbuf[c // 2, 0], vbuf[c // 2, 1]], axis=1)
-            acc = acc + jnp.dot(v, w.astype(jnp.bfloat16), preferred_element_type=jnp.float32)
+            light = w.astype(jnp.bfloat16)
+            for e in (0, 1):
+                acc = acc + jnp.dot(
+                    vbuf[c // 2, e], light[e * R : (e + 1) * R], preferred_element_type=jnp.float32
+                )
         part[b, h] = acc
         stats[b, h, 1:2] = total
 
@@ -222,8 +230,8 @@
     def came(way, s, h):
         return in_s[way, s, h, 0:1], in_s[way, s, h, 1:2], in_o[way, s, h].astype(jnp.float32)
 
-    def back(way, s, h):
-        hlp = 2 * ((z + 1 + (NZ - 2) * way) % NZ) + ylo
+    def back(way, s, h, hop=1):
+        hlp = 2 * ((z + hop + (NZ - 2 * hop) * way) % NZ) + ylo
         return (
             remote(out_o.at[way, s, h], in_o.at[way, s, h], o_send.at[way, s, h], o_recv.at[way, s, h], i, hlp),
             remote(out_s.at[way, s, h], in_s.at[way, s, h], t_send.at[way, s, h], t_recv.at[way, s, h], i, hlp),
@@ -233,11 +241,11 @@
         for copy in back(way, s, h):
             copy.wait_recv()
 
-    def give(way, s, h, state):
+    def give(way, s, h, state, hop=1):
         out_s[way, s, h, 0:1] = state[0]
         out_s[way, s, h, 1:2] = state[1]
         out_o[way, s, h] = state[2].astype(jnp.bfloat16)
-        for copy in back(way, s, h):
+        for copy in back(way, s, h, hop):
             copy.start()
 
     def turn(m, carry):
@@ -248,21 +256,30 @@
         for e in (0, 1):
             attend(b, 2 * c + e)
 
+        heads = (2 * c, 2 * c + 1)
+
         @pl.when(n == 0)
         def _():
-            for e in (0, 1):
-                give(c, 0, 2 * c + e, mine(b, 2 * c + e))
-
-        @pl.when(((n == 1) | (n == 2)) & (c != way))
+            for h in heads:
+                give(c, 0, h, mine(b, h), 2)
+
+        @pl.when((n == 1) | (n == 2))
         def _():
-            for e in (0, 1):
-                give(way, s, 2 * c + e, mine(b, 2 * c + e))
-
-        @pl.when((n < NZ - 1) & ((n > 2) | ((n > 0) & (c == way))))
+            for h in heads:
+                give(way, s, h, mine(b, h))
+
+        @pl.when((n > 2) & (n < NZ - 1) & ((n > 4) | (c != way)))
         def _():
-            for e in (0, 1):
-                landed(way, s - 1, 2 * c + e)
-                give(way, s, 2 * c + e, merge(mine(b, 2 * c + e), came(way, s - 1, 2 * c + e)))
+            for h in heads:
+                landed(way, s - 1, h)
+                give(way, s, h, merge(mine(b, h), came(way, s - 1, h)))
+
+        @pl.when(((n == 3) | (n == 4)) & (c == way))
+        def _():
+            for h in heads:
+                landed(way, 0, h)
+                landed(way, 1, h)
+                give(way, 2, h, merge(merge(mine(b, h), came(way, 0, h)), came(way, 1, h)))
 
         return carry
 
@@ -301,7 +318,7 @@
         out_specs=pl.BlockSpec(memory_space=pltpu.VMEM),
         scratch_shapes=[
             pltpu.VMEM((R, 2 * G * D), bf16),
-            pltpu.VMEM((G, 2, R, D), bf16),
+            pltpu.VMEM((G, D, R), bf16),
             pltpu.VMEM((PAIRS, 2, R, D), bf16),
             pltpu.VMEM((PAIRS, 2, D, R), bf16),
             pltpu.VMEM((NZ, R, HEADS * D), bf16),

time: 54.4 us -> 52.8 us (0.971)
  Pallas kernels: 52.6 us -> 50.8 us
    pallas_call x1, Pallas kernels: 52.6 us -> 50.8 us  [local(): pl.pallas_call(kernel, out_shape=jax.ShapeDtypeStruct((R, HEADS * D), f32...]
where the time goes in v5:
time: 52.8 us; the launch traced here: 52.5 us
  Pallas kernels  50.8 us (96%)
  local copies, waits for them, and re-layouts  1.67 us (3%)
    pallas_call x1, Pallas kernels, local(): pl.pallas_call(kernel, out_shape=jax.ShapeDtypeStruct((R, HEADS * D), f32...  50.8 us
    unnamed x1, local copies, waits for them, and re-layouts  1.67 us

profile of v5, /device:TPU:1, one launch (start us, length us, event | category | flops | bytes accessed | tf_op | source)
XLA Modules:
  0.0 52.5 jit_solution(1094812858263247262)
XLA Ops:
  0.0 50.8 %shard_map.46 = f32[128,512]{1,0:T(8,128)} custom-call(bf16[128,512]{1,0:T(8,128)(2,1)} %q_ref.1, bf16[128,2048]{1,0:T(8,128)(2,1)} %kv_ref.1, s32[1,8,64]{2,1,0:T(8,128)} %bitcast.1, bf16[128,2048]{1,0:T(8,128)(2,1)} %own_ref.1), custom_call_target="tpu_custom_call" | custom-call | tf_op jit(solution)/shard_map/pallas_call | solution.py:314
  50.8 1.7 %copy.6 = f32[128,512]{1,0:T(8,128)} copy(f32[128,512]{1,0:T(8,128)} %shard_map.46) | data formatting | bytes 524288

commit v6 on v5

--- a/solution.py
+++ b/solution.py
@@ -13,9 +13,9 @@
 NZ = 8
 TOPK = 8
 HEADS = 4
-PAIRS = 16
 PLANE = 16
 PIECES = 4
+TAIL = 16
 FAR = -1e9
 SCALE = math.log2(math.e) / math.sqrt(D)
 MESH = pl.DeviceIdType.MESH
@@ -32,9 +32,9 @@
 def kernel(
     q_ref, kv_ref, sel_ref, own_ref, out_ref,
     kvl, vts, kbuf, vbuf, qbuf, sell, selv, sels, ownk, ownv, scores, part, stats, near, nstat,
-    out_o, in_o, out_s, in_s,
+    out_o, in_o,
     loc_sem, k_send, k_recv, f_send, f_recv,
-    q_send, q_recv, s_send, s_recv, o_send, o_recv, t_send, t_recv,
+    q_send, q_recv, s_send, s_recv, o_send, o_recv,
 ):
     i = lax.axis_index("blk")
     j = lax.axis_index("help")
@@ -109,11 +109,11 @@
         t = (me + k) % PLANE
         b, h = plane_of(t)
         src = vts.at[t // 2] if e else kvl.at[:, pl.ds(pl.multiple_of((t // 2) * D, D), D)]
-        return remote(src, held[e].at[i, ylo], k_send.at[e, k], k_recv.at[e, me], b, h)
-
-    def forward(s, e):
-        block = held[e].at[2 * (s // 2) + u, s % 2]
-        return remote(block, block, f_send.at[e, s], f_recv.at[e, s], sib, j)
+        return remote(src, held[e].at[g, u, ylo], k_send.at[e, k], k_recv.at[e, me], b, h)
+
+    def forward(part_of, e):
+        block = held[e].at[pl.ds(part_of * (G // 2), G // 2), u]
+        return remote(block, block, f_send.at[e, part_of], f_recv.at[e, part_of], sib, j)
 
     def s_copy(k):
         h = 2 * ((z + k) % NZ) + ylo
@@ -122,29 +122,28 @@
     lax.fori_loop(1, PLANE, lambda k, c: (kv_copy(k, 0).start(), c)[1], 0)
     selv[z] = jnp.concatenate([sell[...], jnp.zeros((TOPK, D - sell.shape[1]), jnp.int32)], axis=1)
     lax.fori_loop(1, NZ, lambda k, c: (s_copy(k).start(), c)[1], 0)
-    kbuf[i, ylo] = kvl[:, pl.ds(gcol, D)]
-    forward(me, 0).start()
+    kbuf[g, u, ylo] = kvl[:, pl.ds(gcol, D)]
     for head in range(G):
         vts[head] = jnp.transpose(kvl[:, (G + head) * D : (G + head + 1) * D])
-    vbuf[i, ylo] = vts[g]
+    vbuf[g, u, ylo] = vts[g]
 
     def arrive(e):
-        def one(k, c):
-            s = (me + PLANE - k) % PLANE
-            block = held[e].at[2 * (s // 2) + u, s % 2]
-            remote(block, block, k_send.at[e, k], k_recv.at[e, s], sib, j).wait_recv()
-            forward(s, e).start()
+        def one(s, c):
+            @pl.when(s != me)
+            def _():
+                block = held[e].at[s // 2, u, s % 2]
+                remote(block, block, k_send.at[e, 0], k_recv.at[e, s], sib, j).wait_recv()
+
             return c
 
-        lax.fori_loop(1, PLANE, one, 0)
+        for part_of in (0, 1):
+            lax.fori_loop(part_of * (PLANE // 2), (part_of + 1) * (PLANE // 2), one, 0)
+            forward(part_of, e).start()
 
     def from_sibling(e):
-        def one(s, c):
-            block = held[e].at[2 * (s // 2) + (1 - u), s % 2]
-            remote(block, block, f_send.at[e, s], f_recv.at[e, s], sib, j).wait_recv()
-            return c
-
-        lax.fori_loop(0, PLANE, one, 0)
+        for part_of in (0, 1):
+            block = held[e].at[pl.ds(part_of * (G // 2), G // 2), 1 - u]
+            remote(block, block, f_send.at[e, part_of], f_recv.at[e, part_of], sib, j).wait_recv()
 
     def picks_came(k, c):
         zs = (z + NZ - k) % NZ
@@ -153,7 +152,6 @@
 
     q_pass_on(1)
     lax.fori_loop(1, PLANE, lambda k, c: (kv_copy(k, 1).start(), c)[1], 0)
-    forward(me, 1).start()
     lax.fori_loop(1, NZ, picks_came, 0)
     to_smem = pltpu.make_async_copy(selv, sels, loc_sem.at[0])
     to_smem.start()
@@ -185,7 +183,7 @@
             top = jnp.full((1, R), 4 * FAR, jnp.float32)
             for t in range(TOPK):
                 c = sels[b, t, lead + h]
-                k = kbuf[c // 2].reshape(2 * R, D)
+                k = kbuf[c // 4, c // 2 % 2].reshape(2 * R, D)
                 s = lax.dot_general(k, q, NT, preferred_element_type=jnp.float32)
                 scores[b, h, t] = s
                 bias = jnp.where(c % 2 == parity, 0.0, FAR)
@@ -213,7 +211,7 @@
             light = w.astype(jnp.bfloat16)
             for e in (0, 1):
                 acc = acc + jnp.dot(
-                    vbuf[c // 2, e], light[e * R : (e + 1) * R], preferred_element_type=jnp.float32
+                    vbuf[c // 4, c // 2 % 2, e], light[e * R : (e + 1) * R], preferred_element_type=jnp.float32
                 )
         part[b, h] = acc
         stats[b, h, 1:2] = total
@@ -227,26 +225,42 @@
     def mine(b, h):
         return stats[b, h, 0:1], stats[b, h, 1:2], part[b, h]
 
+    def thirds(x):
+        hi = x.astype(jnp.bfloat16).astype(jnp.float32)
+        mid = (x - hi).astype(jnp.bfloat16).astype(jnp.float32)
+        return [hi, mid, x - hi - mid]
+
     def came(way, s, h):
-        return in_s[way, s, h, 0:1], in_s[way, s, h, 1:2], in_o[way, s, h].astype(jnp.float32)
+        rows = in_o[way, s, h, D:].astype(jnp.float32)
+        return (
+            rows[0:1] + rows[1:2] + rows[2:3], rows[3:4] + rows[4:5] + rows[5:6],
+            in_o[way, s, h, :D].astype(jnp.float32),
+        )
 
     def back(way, s, h, hop=1):
         hlp = 2 * ((z + hop + (NZ - 2 * hop) * way) % NZ) + ylo
-        return (
-            remote(out_o.at[way, s, h], in_o.at[way, s, h], o_send.at[way, s, h], o_recv.at[way, s, h], i, hlp),
-            remote(out_s.at[way, s, h], in_s.at[way, s, h], t_send.at[way, s, h], t_recv.at[way, s, h], i, hlp),
+        return remote(
+            out_o.at[way, s, h], in_o.at[way, s, h], o_send.at[way, s, h], o_recv.at[way, s, h], i, hlp
         )
 
     def landed(way, s, h):
-        for copy in back(way, s, h):
-            copy.wait_recv()
+        back(way, s, h).wait_recv()
 
     def give(way, s, h, state, hop=1):
-        out_s[way, s, h, 0:1] = state[0]
-        out_s[way, s, h, 1:2] = state[1]
-        out_o[way, s, h] = state[2].astype(jnp.bfloat16)
-        for copy in back(way, s, h, hop):
-            copy.start()
+        rows = jnp.concatenate(thirds(state[0]) + thirds(state[1]) + [jnp.zeros((TAIL - 6, R), jnp.float32)], axis=0)
+        out_o[way, s, h, :D] = state[2].astype(jnp.bfloat16)
+        out_o[way, s, h, D:] = rows.astype(jnp.bfloat16)
+        back(way, s, h, hop).start()
+
+    def all_have_left():
+        for s in range(1, 5):
+            for w, p in q_steps(s):
+                q_copy(w, s, p).wait_send()
+        for e in (0, 1):
+            lax.fori_loop(1, PLANE, lambda k, c: (kv_copy(k, e).wait_send(), c)[1], 0)
+            for part_of in (0, 1):
+                forward(part_of, e).wait_send()
+        lax.fori_loop(1, NZ, lambda k, c: (s_copy(k).wait_send(), c)[1], 0)
 
     def turn(m, carry):
         n, c = m // 2, m % 2
@@ -258,6 +272,10 @@
 
         heads = (2 * c, 2 * c + 1)
 
+        @pl.when(m == 6)
+        def _():
+            all_have_left()
+
         @pl.when(n == 0)
         def _():
             for h in heads:
@@ -292,19 +310,11 @@
             state = merge(state, came(way, 3, h))
         out_ref[:, h * D : (h + 1) * D] = jnp.transpose(state[2] / state[1])
 
-    for s in range(1, 5):
-        for w, p in q_steps(s):
-            q_copy(w, s, p).wait_send()
-    for e in (0, 1):
-        lax.fori_loop(1, PLANE, lambda k, c: (kv_copy(k, e).wait_send(), c)[1], 0)
-        lax.fori_loop(0, PLANE, lambda k, c: (forward(k, e).wait_send(), c)[1], 0)
-    lax.fori_loop(1, NZ, lambda k, c: (s_copy(k).wait_send(), c)[1], 0)
     for s in range(4):
         for way in (0, 1):
             for h in range(HEADS):
                 if s > 0 or h // 2 == way:
-                    for copy in back(way, s, h):
-                        copy.wait_send()
+                    back(way, s, h).wait_send()
 
 
 def local(queries, query_key_value, cached_key_value, selected):
@@ -319,10 +329,10 @@
         scratch_shapes=[
             pltpu.VMEM((R, 2 * G * D), bf16),
             pltpu.VMEM((G, D, R), bf16),
-            pltpu.VMEM((PAIRS, 2, R, D), bf16),
-            pltpu.VMEM((PAIRS, 2, D, R), bf16),
+            pltpu.VMEM((G, 2, 2, R, D), bf16),
+            pltpu.VMEM((G, 2, 2, D, R), bf16),
             pltpu.VMEM((NZ, R, HEADS * D), bf16),
-            pltpu.VMEM((TOPK, PAIRS * HEADS), jnp.int32),
+            pltpu.VMEM((TOPK, PLANE * HEADS), jnp.int32),
             pltpu.VMEM((NZ, TOPK, D), jnp.int32),
             pltpu.SMEM((NZ, TOPK, D), jnp.int32),
             pltpu.VMEM((R, D), bf16),
@@ -332,15 +342,13 @@
             pltpu.VMEM((NZ, HEADS, 8, R), f32),
             pltpu.VMEM((HEADS, D, R), f32),
             pltpu.VMEM((HEADS, 8, R), f32),
-            pltpu.VMEM((2, 4, HEADS, D, R), bf16),
-            pltpu.VMEM((2, 4, HEADS, D, R), bf16),
-            pltpu.VMEM((2, 4, HEADS, 8, R), f32),
-            pltpu.VMEM((2, 4, HEADS, 8, R), f32),
+            pltpu.VMEM((2, 4, HEADS, D + TAIL, R), bf16),
+            pltpu.VMEM((2, 4, HEADS, D + TAIL, R), bf16),
             dma((5,)),
-            dma((2, PLANE)), dma((2, PLANE)), dma((2, PLANE)), dma((2, PLANE)),
+            dma((2, PLANE)), dma((2, PLANE)), dma((2, 2)), dma((2, 2)),
             dma((2, 4, PIECES)), dma((2, 4, PIECES)),
             dma((NZ,)), dma((NZ,)),
-            dma((2, 4, HEADS)), dma((2, 4, HEADS)), dma((2, 4, HEADS)), dma((2, 4, HEADS)),
+            dma((2, 4, HEADS)), dma((2, 4, HEADS)),
         ],
         compiler_params=pltpu.CompilerParams(
             collective_id=0, has_side_effects=True, vmem_limit_bytes=58 * 2**20

time: 52.8 us -> 51.9 us (0.983); the launches traced: 52.5 us -> 50.9 us
  Pallas kernels: 50.8 us -> 49.2 us
    pallas_call x1, Pallas kernels: 50.8 us -> 49.2 us  [local(): pl.pallas_call(kernel, out_shape=jax.ShapeDtypeStruct((R, HEADS * D), f32...]
where the time goes in v6:
time: 51.9 us; the launch traced here: 50.9 us
  Pallas kernels  49.2 us (95%)
  local copies, waits for them, and re-layouts  1.67 us (3%)
    pallas_call x1, Pallas kernels, local(): pl.pallas_call(kernel, out_shape=jax.ShapeDtypeStruct((R, HEADS * D), f32...  49.2 us
    unnamed x1, local copies, waits for them, and re-layouts  1.67 us

profile of v6, /device:TPU:1, one launch (start us, length us, event | category | flops | bytes accessed | tf_op | source)
XLA Modules:
  0.0 50.9 jit_solution(4699303149549601164)
XLA Ops:
  0.0 49.2 %shard_map.46 = f32[128,512]{1,0:T(8,128)} custom-call(bf16[128,512]{1,0:T(8,128)(2,1)} %q_ref.1, bf16[128,2048]{1,0:T(8,128)(2,1)} %kv_ref.1, s32[1,8,64]{2,1,0:T(8,128)} %bitcast.1, bf16[128,2048]{1,0:T(8,128)(2,1)} %own_ref.1), custom_call_target="tpu_custom_call" | custom-call | tf_op jit(solution)/shard_map/pallas_call | solution.py:324
  49.2 1.7 %copy.6 = f32[128,512]{1,0:T(8,128)} copy(f32[128,512]{1,0:T(8,128)} %shard_map.46) | data formatting | bytes 524288

commit v7 on v6

--- a/solution.py
+++ b/solution.py
@@ -151,11 +151,11 @@
         return c
 
     q_pass_on(1)
-    lax.fori_loop(1, PLANE, lambda k, c: (kv_copy(k, 1).start(), c)[1], 0)
     lax.fori_loop(1, NZ, picks_came, 0)
     to_smem = pltpu.make_async_copy(selv, sels, loc_sem.at[0])
     to_smem.start()
     q_pass_on(2)
+    lax.fori_loop(1, PLANE, lambda k, c: (kv_copy(k, 1).start(), c)[1], 0)
     arrive(0)
 
     causal = lax.broadcasted_iota(jnp.int32, (R, R), 0) <= lax.broadcasted_iota(jnp.int32, (R, R), 1)

time: 51.9 us -> 50.4 us (0.971)
  Pallas kernels: 49.2 us -> 48.1 us
    pallas_call x1, Pallas kernels: 49.2 us -> 48.1 us  [local(): pl.pallas_call(kernel, out_shape=jax.ShapeDtypeStruct((R, HEADS * D), f32...]
where the time goes in v7:
time: 50.4 us; the launch traced here: 49.8 us
  Pallas kernels  48.1 us (95%)
  local copies, waits for them, and re-layouts  1.67 us (3%)
    pallas_call x1, Pallas kernels, local(): pl.pallas_call(kernel, out_shape=jax.ShapeDtypeStruct((R, HEADS * D), f32...  48.1 us
    unnamed x1, local copies, waits for them, and re-layouts  1.67 us

profile of v7, /device:TPU:1, one launch (start us, length us, event | category | flops | bytes accessed | tf_op | source)
XLA Modules:
  0.0 49.8 jit_solution(11277371424043181737)
XLA Ops:
  0.0 48.1 %shard_map.46 = f32[128,512]{1,0:T(8,128)} custom-call(bf16[128,512]{1,0:T(8,128)(2,1)} %q_ref.1, bf16[128,2048]{1,0:T(8,128)(2,1)} %kv_ref.1, s32[1,8,64]{2,1,0:T(8,128)} %bitcast.1, bf16[128,2048]{1,0:T(8,128)(2,1)} %own_ref.1), custom_call_target="tpu_custom_call" | custom-call | tf_op jit(solution)/shard_map/pallas_call | solution.py:324
  48.2 1.7 %copy.6 = f32[128,512]{1,0:T(8,128)} copy(f32[128,512]{1,0:T(8,128)} %shard_map.46) | data formatting | bytes 524288

commit v8 on v7

--- a/solution.py
+++ b/solution.py
@@ -14,7 +14,7 @@
 TOPK = 8
 HEADS = 4
 PLANE = 16
-PIECES = 4
+PIECES = 8
 TAIL = 16
 FAR = -1e9
 SCALE = math.log2(math.e) / math.sqrt(D)
@@ -164,9 +164,9 @@
         s = lax.dot_general(
             ownk[...], qbuf[z, :, h * D : (h + 1) * D], NT, preferred_element_type=jnp.float32
         )
-        s = jnp.where(causal, s, FAR)
+        s = jnp.where(causal, s * SCALE, FAR)
         top = jnp.max(s, axis=0, keepdims=True)
-        w = jnp.exp2((s - top) * SCALE)
+        w = jnp.exp2(s - top)
         nstat[h, 0:1] = top
         nstat[h, 1:2] = jnp.sum(w, axis=0, keepdims=True)
         near[h] = jnp.dot(own_vt, w.astype(jnp.bfloat16), preferred_element_type=jnp.float32)
@@ -180,15 +180,15 @@
     def score(b, carry):
         for h in range(HEADS):
             q = qbuf[b, :, h * D : (h + 1) * D]
-            top = jnp.full((1, R), 4 * FAR, jnp.float32)
+            top = jnp.full((8, R), 4 * FAR, jnp.float32)
             for t in range(TOPK):
                 c = sels[b, t, lead + h]
                 k = kbuf[c // 4, c // 2 % 2].reshape(2 * R, D)
-                s = lax.dot_general(k, q, NT, preferred_element_type=jnp.float32)
+                s = lax.dot_general(k, q, NT, preferred_element_type=jnp.float32) * SCALE
                 scores[b, h, t] = s
                 bias = jnp.where(c % 2 == parity, 0.0, FAR)
-                top = jnp.maximum(top, jnp.max(s, axis=0, keepdims=True) + bias)
-            stats[b, h, 0:1] = top
+                top = jnp.maximum(top, jnp.max(s.reshape(2 * R // 8, 8, R), axis=0) + bias)
+            stats[b, h, 0:1] = jnp.max(top, axis=0, keepdims=True)
         return carry
 
     lax.fori_loop(0, NZ - 3, lambda n, c: score((z + 6 + n) % NZ, c), 0)
@@ -201,25 +201,25 @@
 
     def attend(b, h):
         top = stats[b, h, 0:1]
-        total = jnp.zeros((1, R), jnp.float32)
+        total = jnp.zeros((8, R), jnp.float32)
         acc = jnp.zeros((D, R), jnp.float32)
         for t in range(TOPK):
             c = sels[b, t, lead + h]
-            level = jnp.where(c % 2 == parity, top * SCALE, -FAR)
-            w = jnp.exp2(scores[b, h, t] * SCALE - level)
-            total = total + jnp.sum(w, axis=0, keepdims=True)
+            level = jnp.where(c % 2 == parity, top, -FAR)
+            w = jnp.exp2(scores[b, h, t] - level)
+            total = total + jnp.sum(w.reshape(2 * R // 8, 8, R), axis=0)
             light = w.astype(jnp.bfloat16)
             for e in (0, 1):
                 acc = acc + jnp.dot(
                     vbuf[c // 4, c // 2 % 2, e], light[e * R : (e + 1) * R], preferred_element_type=jnp.float32
                 )
         part[b, h] = acc
-        stats[b, h, 1:2] = total
+        stats[b, h, 1:2] = jnp.sum(total, axis=0, keepdims=True)
 
     def merge(a, b):
         (ma, la, oa), (mb, lb, ob) = a, b
         m = jnp.maximum(ma, mb)
-        fa, fb = jnp.exp2((ma - m) * SCALE), jnp.exp2((mb - m) * SCALE)
+        fa, fb = jnp.exp2(ma - m), jnp.exp2(mb - m)
         return m, la * fa + lb * fb, oa * fa + ob * fb
 
     def mine(b, h):
@@ -229,6 +229,9 @@
         hi = x.astype(jnp.bfloat16).astype(jnp.float32)
         mid = (x - hi).astype(jnp.bfloat16).astype(jnp.float32)
         return [hi, mid, x - hi - mid]
+
+    def keep(h, state):
+        stats[z, h, 0:1], stats[z, h, 1:2], part[z, h] = state
 
     def came(way, s, h):
         rows = in_o[way, s, h, D:].astype(jnp.float32)
@@ -266,15 +269,10 @@
         n, c = m // 2, m % 2
         s = (n + 1) // 2
         way = (n + 1) % 2
-        b = jnp.where(n == NZ - 1, z, jnp.where(way == 0, z + 4 - s, z + 4 + s) % NZ)
-        for e in (0, 1):
-            attend(b, 2 * c + e)
-
+        b = jnp.where(way == 0, z + 4 - s, z + 4 + s) % NZ
         heads = (2 * c, 2 * c + 1)
-
-        @pl.when(m == 6)
-        def _():
-            all_have_left()
+        for h in heads:
+            attend(b, h)
 
         @pl.when(n == 0)
         def _():
@@ -286,25 +284,29 @@
             for h in heads:
                 give(way, s, h, mine(b, h))
 
-        @pl.when((n > 2) & (n < NZ - 1) & ((n > 4) | (c != way)))
-        def _():
-            for h in heads:
-                landed(way, s - 1, h)
-                give(way, s, h, merge(mine(b, h), came(way, s - 1, h)))
-
-        @pl.when(((n == 3) | (n == 4)) & (c == way))
-        def _():
-            for h in heads:
+        return carry
+
+    lax.fori_loop(0, 2 * (NZ - 1), turn, 0)
+    all_have_left()
+    for h in range(HEADS):
+        for way in (0, 1):
+            b = at((2 - 4 * way))
+            state = mine(b, h)
+            if h // 2 == way:
                 landed(way, 0, h)
-                landed(way, 1, h)
-                give(way, 2, h, merge(merge(mine(b, h), came(way, 0, h)), came(way, 1, h)))
-
-        return carry
-
-    lax.fori_loop(0, 2 * NZ, turn, 0)
-
-    for h in range(HEADS):
-        state = merge(mine(z, h), (nstat[h, 0:1], nstat[h, 1:2], near[h]))
+                state = merge(state, came(way, 0, h))
+            landed(way, 1, h)
+            give(way, 2, h, merge(state, came(way, 1, h)))
+    lax.fori_loop(0, HEADS, lambda h, c: (attend(z, h), c)[1], 0)
+    for h in range(HEADS):
+        keep(h, merge(mine(z, h), (nstat[h, 0:1], nstat[h, 1:2], near[h])))
+    for h in range(HEADS):
+        for way in (0, 1):
+            landed(way, 2, h)
+            give(way, 3, h, merge(mine(at(1 - 2 * way), h), came(way, 2, h)))
+
+    for h in range(HEADS):
+        state = mine(z, h)
         for way in (0, 1):
             landed(way, 3, h)
             state = merge(state, came(way, 3, h))

time: 50.4 us -> 50.1 us (level)
  no operation moved by 1% of the time
where the time goes in v8:
time: 50.1 us; the launch traced here: 50 us
  Pallas kernels  48.3 us (96%)
  local copies, waits for them, and re-layouts  1.67 us (3%)
    pallas_call x1, Pallas kernels, local(): pl.pallas_call(kernel, out_shape=jax.ShapeDtypeStruct((R, HEADS * D), f32...  48.3 us
    unnamed x1, local copies, waits for them, and re-layouts  1.67 us

profile of v8, /device:TPU:1, one launch (start us, length us, event | category | flops | bytes accessed | tf_op | source)
XLA Modules:
  0.0 50.0 jit_solution(15289543966044054996)
XLA Ops:
  0.0 48.3 %shard_map.46 = f32[128,512]{1,0:T(8,128)} custom-call(bf16[128,512]{1,0:T(8,128)(2,1)} %q_ref.1, bf16[128,2048]{1,0:T(8,128)(2,1)} %kv_ref.1, s32[1,8,64]{2,1,0:T(8,128)} %bitcast.1, bf16[128,2048]{1,0:T(8,128)(2,1)} %own_ref.1), custom_call_target="tpu_custom_call" | custom-call | tf_op jit(solution)/shard_map/pallas_call | solution.py:326
  48.3 1.7 %copy.6 = f32[128,512]{1,0:T(8,128)} copy(f32[128,512]{1,0:T(8,128)} %shard_map.46) | data formatting | bytes 524288
